TPU v7x, 512 devices: a whole 4x4x16 slice. The times are simulated.
512 devices in a mesh: member: 8 (over z_hi, core), grid: 64 (over y, z_lo, x).
Axes of the slice: x: 4, y: 4, z: 16 (z_hi: 4, z_lo: 4; z = z_hi * 4 + z_lo), core: 2. Of those that a mesh axis runs over, the one named last changes fastest.
Arguments:
- node_feats: bfloat16 [8, 32768, 1024], P('member', 'grid'), may hold values from -6 to 6
- norm_gain: bfloat16 [1024], replicated, may hold values from 0.099609375 to 1.8984375
- w_query: bfloat16 [1024, 1024], P('grid'), may hold values from -0.1875 to 0.1875
- w_key: bfloat16 [1024, 1024], P('grid'), may hold values from -0.1875 to 0.1875
- w_value: bfloat16 [1024, 1024], P('grid'), may hold values from -0.1875 to 0.1875
- w_out: bfloat16 [1024, 1024], P('grid'), may hold values from -0.1875 to 0.1875
- head_scale: float32 [16], replicated, may hold values from 2 to 600
- w_dec: bfloat16 [100, 1024], replicated, may hold values from -0.1875 to 0.1875
- targets: bfloat16 [100, 65536], P(None, 'grid'), may hold values from -6 to 6
- cell_node: int32 [65536], P('grid'), may hold values from 0 to 511
- cell_area: float32 [65536], P('grid'), may hold values from 0.002 to 0.02
Outputs:
- member_score: float32 [8, 100, 65536], P('member', None, 'grid')
- grad_dec: float32 [100, 1024], replicated
All inputs are finite; a program needn't handle non-finite values.
Results may differ from a plain program's by a relative error of at most 0.0095.
The roundings to bfloat16 on the way count: a program that leaves them out, or rounds other values in their place, can miss the bound.
Values may be sent and summed in bfloat16 or wider, within the bound.
No kernel may reach another device: no remote copies, remote signals or barrier semaphores. Data moves between devices by JAX's collectives and lax.ppermute only.
A program may use at most 64 MiB of HBM per device.

v0:
```python
import jax
import jax.numpy as jnp
from jax import lax
from jax.sharding import PartitionSpec as P

WIN = 512


EPS = 1e-06
SMOOTH_SQ = 0.0625
ALPHA = 0.95
GROUP = 4


def extended(x, sides, width):
    for axis, dim in sides:
        devices, length = (lax.axis_size(axis), x.shape[dim])
        up = [(i, (i + 1) % devices) for i in range(devices - 1)]
        down = [(j, i) for i, j in up]
        last = lax.slice_in_dim(x, length - width, length, axis=dim)
        leading = lax.slice_in_dim(x, 0, width, axis=dim)
        before = lax.ppermute(last, axis, up)
        after = lax.ppermute(leading, axis, down)
        x = jnp.concatenate([before, x, after], axis=dim)
    return x


def shifted(value, axis, steps):
    count = lax.axis_size(axis)
    pairs = [(source, (source + steps) % count) for source in range(count)]
    return lax.ppermute(value, axis, pairs)


def rms_norm(features, gain):
    values = features.astype(jnp.float32)
    scale = lax.rsqrt(jnp.mean(values * values, -1, keepdims=True) + EPS)
    return (values * scale * gain.astype(jnp.float32)).astype(jnp.bfloat16)


def unit_rows(tensor):
    return tensor * lax.rsqrt(jnp.sum(tensor * tensor, -1, keepdims=True) + EPS)


def head_groups(tensor, heads, head_dim):
    rows = tensor.shape[0]
    return tensor.reshape(rows, heads // GROUP, GROUP, head_dim).transpose(1, 0, 2, 3)


def body(
    node_feats,
    norm_gain,
    w_query,
    w_key,
    w_value,
    w_out,
    head_scale,
    w_dec,
    targets,
    cell_node,
    cell_area,
):
    features = node_feats[0]
    node_count, width = features.shape
    heads = head_scale.shape[0]
    head_dim = width // heads
    half = WIN // 2
    ext_count = node_count + 2 * half
    normed = rms_norm(features, norm_gain)
    pieces = (
        lax.all_gather(w_query, "grid", axis=0, tiled=True),
        lax.all_gather(w_key, "grid", axis=0, tiled=True),
        lax.all_gather(w_value, "grid", axis=0, tiled=True),
    )
    columns = normed
    query_raw, keys_raw, values_raw = tuple(
        (jnp.dot(columns, pieces[idx], preferred_element_type=jnp.float32) for idx in range(3))
    )
    shaped = query_raw.reshape(node_count, heads, head_dim)
    query = (unit_rows(shaped) * head_scale[None, :, None]).astype(jnp.bfloat16)
    keys_own = (
        unit_rows(keys_raw.reshape(node_count, heads, head_dim))
        .astype(jnp.bfloat16)
        .reshape(node_count, width)
    )
    keyval = jnp.concatenate([keys_own, values_raw.astype(jnp.bfloat16)], axis=1)
    keyval_ext = extended(keyval, (("grid", 0),), half)
    keys_ext = keyval_ext[:, :width].reshape(ext_count, heads, head_dim)
    values_ext = keyval_ext[:, width:].reshape(ext_count, heads, head_dim)
    total_nodes = node_count * lax.axis_size("grid")
    base = lax.axis_index("grid") * node_count
    query_pos = base + jnp.arange(node_count, dtype=jnp.int32)
    key_pos = base - half + jnp.arange(ext_count, dtype=jnp.int32)
    offset = key_pos[None, :] - query_pos[:, None]
    allowed = (
        (offset >= -half)
        & (offset < half)
        & (key_pos >= 0)[None, :]
        & (key_pos < total_nodes)[None, :]
    )

    def attend(group_arrays):
        query_grp, keys_grp, values_grp = group_arrays
        score = jnp.einsum("nhd,ehd->hne", query_grp, keys_grp, preferred_element_type=jnp.float32)
        score = jnp.where(allowed[None], score, -jnp.inf)
        top = jnp.max(score, -1, keepdims=True)
        expo = jnp.exp(score - top)
        weights = (expo / jnp.sum(expo, -1, keepdims=True)).astype(jnp.bfloat16)
        return jnp.einsum("hne,ehd->nhd", weights, values_grp, preferred_element_type=jnp.float32)

    grouped = lax.map(
        attend,
        (
            head_groups(query, heads, head_dim),
            head_groups(keys_ext, heads, head_dim),
            head_groups(values_ext, heads, head_dim),
        ),
    )
    attended = grouped.transpose(1, 0, 2, 3).reshape(node_count, width).astype(jnp.bfloat16)
    columns = attended
    projected = jnp.dot(
        columns,
        lax.all_gather(w_out, "grid", axis=0, tiled=True),
        preferred_element_type=jnp.float32,
    )
    hidden = (features.astype(jnp.float32) + projected).astype(jnp.bfloat16)
    node_out = lax.dot_general(
        w_dec, hidden, (((1,), (1,)), ((), ())), preferred_element_type=jnp.float32
    )
    fields = jnp.take(node_out, cell_node, axis=1).astype(jnp.bfloat16)
    own = fields.astype(jnp.float32)
    members = lax.axis_size("member")
    spread = jnp.zeros_like(own)
    slope = jnp.zeros_like(own)
    moving = fields
    for turn in range(members - 1):
        moving = shifted(moving, "member", 1)
        delta = own - moving.astype(jnp.float32)
        smooth = jnp.sqrt(delta * delta + SMOOTH_SQ)
        spread = spread + smooth
        slope = slope + delta / smooth
    kappa = ALPHA / (2.0 * members * (members - 1)) + (1.0 - ALPHA) / (2.0 * members * members)
    truth = targets.astype(jnp.float32)
    error = own - truth
    error_s = jnp.sqrt(error * error + SMOOTH_SQ)
    member_score = error_s / members - kappa * spread
    cell_grad = cell_area[None, :] * (error / error_s / members - 2.0 * kappa * slope)
    one_hot = (cell_node[:, None] == jnp.arange(node_count, dtype=jnp.int32)[None, :]).astype(
        jnp.float32
    )
    node_grad = jnp.dot(cell_grad, one_hot, precision=lax.Precision.HIGHEST).astype(jnp.bfloat16)
    local_grad = jnp.dot(node_grad, hidden, preferred_element_type=jnp.float32)
    grad_dec = lax.psum(local_grad, ("member", "grid"))
    return (member_score[None], grad_dec)


def solution(mesh):
    in_specs = (
        P("member", "grid", None),
        P(),
        P("grid", None),
        P("grid", None),
        P("grid", None),
        P("grid", None),
        P(),
        P(),
        P(None, "grid"),
        P("grid"),
        P("grid"),
    )
    out_specs = (P("member", None, "grid"), P())
    return jax.shard_map(body, mesh=mesh, in_specs=in_specs, out_specs=out_specs, check_vma=False)
```

profile of v0, /device:TPU:1, one launch (start us, length us, event | category | flops | bytes accessed | tf_op | source)
XLA Modules:
  0.0 2007.4 jit_solution(5490552223403663668)
XLA Ops:
  13.6 312.2 %all-gather.5.cloned.1.call-done = bf16[1024,1024]{1,0:T(8,128)(2,1)} async-done(((bf16[16,1024]{1,0:T(8,128)(2,1)}), bf16[1024,1024]{1,0:T(8,128)(2,1)}) %all-gather.5.cloned.1.call-update) | async-done | bytes 2097168 | tf_op jit(solution)/shard_map/all_gather | solution.py:71
  331.0 349.6 %all-gather.7.cloned.1.call-done = bf16[1024,1024]{1,0:T(8,128)(2,1)} async-done(((bf16[16,1024]{1,0:T(8,128)(2,1)}), bf16[1024,1024]{1,0:T(8,128)(2,1)}) %all-gather.7.cloned.1.call-update) | async-done | bytes 2097168 | tf_op jit(solution)/shard_map/all_gather | solution.py:72
  689.2 346.2 %all-gather.9.cloned.1.call-done = bf16[1024,1024]{1,0:T(8,128)(2,1)} async-done(((bf16[16,1024]{1,0:T(8,128)(2,1)}), bf16[1024,1024]{1,0:T(8,128)(2,1)}) %all-gather.9.cloned.1.call-update) | async-done | bytes 2097168 | tf_op jit(solution)/shard_map/all_gather | solution.py:70
  1054.9 55.3 %while.11 = (s32[]{:T(128)}, bf16[4,512,4,64]{1,3,2,0:T(8,128)(2,1)}, bf16[4,1024,4,64]{1,3,2,0:T(8,128)(2,1)}, bf16[4,512,4,64]{1,3,2,0:T(8,128)(2,1)}, bf16[4,...) while((s32[]{:T(128)}, ...), condition=%wide.region_6.7_spmd.clone, body=%wide.region_3.6_spmd.clone.sunk | while | flops 550503424 | bytes 28076188 | solution.py:110
  1055.6 7.1 fusion.123
  1062.7 5.0 fusion.124
  1069.4 7.1 fusion.123
  1076.5 5.0 fusion.124
  1083.2 7.1 fusion.123
  1097.0 7.1 fusion.123
  1104.1 5.0 fusion.124
  1110.1 279.9 %all-gather.11.cloned.1.call-done = bf16[1024,1024]{1,0:T(8,128)(2,1)} async-done(((bf16[16,1024]{1,0:T(8,128)(2,1)}), bf16[1024,1024]{1,0:T(8,128)(2,1)}) %all-gather.11.cloned.1.call-update) | async-done | bytes 2097168 | tf_op jit(solution)/shard_map/all_gather | solution.py:122
  1397.3 52.2 %collective-permute-start.2 = (bf16[100,1024]{0,1:T(8,128)(2,1)S(1)}, bf16[100,1024]{0,1:T(8,128)(2,1)S(1)}, u32[]{:S(2)}, u32[]{:S(2)}) collective-permute-start(bf16[100,1024]{0,1:T(8,128)(2,1)S(1)} %fusion.82), channel_id=1, source_target_pairs={{0,64},{64,128},{128,192},{192,256},{256,320},{320,384},{384,448},... | collective-permute-start | bytes 614408 | tf_op jit(solution)/shard_map/ppermute | solution.py:31
  1449.5 5.9 collective-permute-done.2
  1455.4 8.4 collective-permute-start.3
  1463.8 6.5 collective-permute-done.3
  1470.3 8.4 collective-permute-start.4
  1478.7 6.8 collective-permute-done.4
  1485.5 8.4 collective-permute-start.5
  1493.9 5.1 collective-permute-done.5
  1499.0 8.4 collective-permute-start.6
  1511.0 8.3 collective-permute-start.7
  1522.6 8.6 collective-permute-start.8
  1543.8 455.2 %all-reduce.2.cloned.1.call-done = f32[100,1024]{1,0:T(8,128)} async-done(((f32[100,1024]{1,0:T(8,128)}), f32[100,1024]{1,0:T(8,128)}) %all-reduce.2.cloned.1.call-update) | async-done | bytes 409616 | tf_op jit(solution)/shard_map/psum | solution.py:152
  (83 shorter events, 79.6 us)
Async XLA Ops:
  7.2 1386.1 %copy-start = (bf16[100,1024]{1,0:T(8,128)(2,1)S(1)}, bf16[100,1024]{1,0:T(8,128)(2,1)}, u32[]{:S(2)}) copy-start(bf16[100,1024]{1,0:T(8,128)(2,1)} %param.20) | copy-start | bytes 614404
  7.2 318.6 %all-gather.5.cloned.1.call-start = ((), (), s32[]{:S(2)}) async-start(), calls=%async_computation | async-start | bytes 2129920 | tf_op jit(solution)/shard_map/all_gather | solution.py:71
  7.9 672.7 %all-gather.7.cloned.1.call-start = ((), (), s32[]{:S(2)}) async-start(), calls=%async_computation.1 | async-start | bytes 2129920 | tf_op jit(solution)/shard_map/all_gather | solution.py:72
  8.7 1026.8 %all-gather.9.cloned.1.call-start = ((), (), s32[]{:S(2)}) async-start(), calls=%async_computation.2 | async-start | bytes 2129920 | tf_op jit(solution)/shard_map/all_gather | solution.py:70
  9.4 1380.6 %all-gather.11.cloned.1.call-start = ((), (), s32[]{:S(2)}) async-start(), calls=%async_computation.3 | async-start | bytes 2129920 | tf_op jit(solution)/shard_map/all_gather | solution.py:122
  10.0 1989.1 %all-reduce.2.cloned.1.call-start = ((), (), s32[]{:S(2)}) async-start(), calls=%async_computation.4 | async-start | bytes 851968 | tf_op jit(solution)/shard_map/psum | solution.py:152
  325.8 3.0 copy-start.1
  685.0 358.7 %collective-permute-start = (bf16[256,2048]{1,0:T(8,128)(2,1)}, bf16[256,2048]{1,0:T(8,128)(2,1)}, u32[]{:S(2)}, u32[]{:S(2)}) collective-permute-start(bf16[256,2048]{1,0:T(8,128)(2,1)} %get-tuple-element.85), channel_id=1, source_target_pairs={{0,1},{1,2},{2,3},{3,4},{4,5},{5,6},{6,7},{7,8},{8,9},{9,10},{10,1... | collective-permute-start | bytes 3145736 | tf_op jit(solution)/shard_map/ppermute | solution.py:22
  687.7 356.1 %collective-permute-start.1 = (bf16[256,2048]{1,0:T(8,128)(2,1)}, bf16[256,2048]{1,0:T(8,128)(2,1)}, u32[]{:S(2)}, u32[]{:S(2)}) collective-permute-start(bf16[256,2048]{1,0:T(8,128)(2,1)} %get-tuple-element.86), channel_id=1, source_target_pairs={{1,0},{2,1},{3,2},{4,3},{5,4},{6,5},{7,6},{8,7},{9,8},{10,9},{11,1... | collective-permute-start | bytes 3145736 | tf_op jit(solution)/shard_map/ppermute | solution.py:23
  1039.3 3.0 copy-start.3
  1055.6 7.1 copy-start.5
  1069.4 7.1 copy-start.5
  1083.2 7.1 copy-start.5
  1095.3 1.0 copy-start.6
  1097.0 7.1 copy-start.5
  1393.2 141.4 %copy-start.2 = (s32[1024]{0:T(1024)S(1)}, s32[1024]{0:T(1024)}, u32[]{:S(2)}) copy-start(s32[1024]{0:T(1024)} %param.22) | copy-start | bytes 12292
  1393.2 141.4 %copy-start.4 = (f32[1024]{0:T(1024)S(1)}, f32[1024]{0:T(1024)}, u32[]{:S(2)}) copy-start(f32[1024]{0:T(1024)} %param.23) | copy-start | bytes 12292
  1397.3 58.1 %collective-permute-start.2 = (bf16[100,1024]{0,1:T(8,128)(2,1)S(1)}, bf16[100,1024]{0,1:T(8,128)(2,1)S(1)}, u32[]{:S(2)}, u32[]{:S(2)}) collective-permute-start(bf16[100,1024]{0,1:T(8,128)(2,1)S(1)} %fusion.82), channel_id=1, source_target_pairs={{0,64},{64,128},{128,192},{192,256},{256,320},{320,384},{384,448},... | collective-permute-start | bytes 614408 | tf_op jit(solution)/shard_map/ppermute | solution.py:31
  1455.4 14.9 collective-permute-start.3
  1470.3 15.2 collective-permute-start.4
  1485.5 13.5 collective-permute-start.5
  1499.0 12.0 collective-permute-start.6
  1511.0 11.6 collective-permute-start.7
  1522.6 12.0 collective-permute-start.8
  (3 other events, 2.9 us)
Sparse Core Ops, SparseCore 0:
  10.1 315.6 all-gather.4
  327.9 352.6 all-gather.6
  682.7 352.6 all-gather.8
  1037.4 352.6 all-gather.10
  1540.1 458.8 all-reduce.1
where the time goes:
time: 2010 us
  waiting for transfers between devices  1780 us (89%)
  starting transfers between devices  107 us (5%)
  matrix products  64.7 us (3%)
  local copies, waits for them, and re-layouts  27 us (1%)
    psum x1, waiting for transfers between devices, body(): grad_dec = lax.psum(local_grad, ('member', 'grid'))  455 us
    all_gather x1, waiting for transfers between devices, body(): lax.all_gather(w_value, 'grid', axis=0, tiled=True)  350 us
    all_gather x1, waiting for transfers between devices, body(): lax.all_gather(w_query, 'grid', axis=0, tiled=True)  346 us
    all_gather x1, waiting for transfers between devices, body(): lax.all_gather(w_key, 'grid', axis=0, tiled=True)  312 us
    all_gather x1, waiting for transfers between devices, body(): lax.all_gather(w_out, 'grid', axis=0, tiled=True)  280 us
    ppermute x7, starting transfers between devices, shifted(): return lax.ppermute(value, axis, pairs)  103 us
  transfers between devices with their start and end apart: 14, of which 12 were waited for; matrix products, arithmetic and copies ran while one was open for 4% of the time, Pallas kernels for 0%

commit v1 on v0

v1 whole, which is shorter than its diff:
```python
import functools

import jax
import jax.numpy as jnp
from jax import lax
from jax.experimental import pallas as pl
from jax.experimental.pallas import tpu as pltpu
from jax.sharding import Mesh, PartitionSpec as P

HALF = 256
EPS = 1e-06
SMOOTH_SQ = 0.0625
ALPHA = 0.95
LANES = 128
BLOCK = 128
LOW = -1e30
MIB = 1024 * 1024

GRID = ("y", "z_lo", "x")
MEMBER = ("z_hi", "core")

f32 = jnp.float32
bf16 = jnp.bfloat16


def dot(a, b):
    return jnp.dot(a, b, preferred_element_type=f32)


def dot_t(a, b):
    return lax.dot_general(a, b, (((1,), (1,)), ((), ())), preferred_element_type=f32)


def halves(x):
    high = x.astype(bf16)
    return high, (x - high.astype(f32)).astype(bf16)


def loop(count, fn):
    def step(i, _):
        fn(i)
        return 0

    lax.fori_loop(0, count, step, 0)


def normalise(before, feats, after, gain, normed):
    gain_row = gain[...].astype(f32)
    start = 0
    for ref in (before, feats, after):

        def norm(i, ref=ref, start=start):
            x = ref[pl.ds(pl.multiple_of(i * 64, 64), 64), :].astype(f32)
            mean = jnp.mean(x * x, -1, keepdims=True)
            y = x * lax.rsqrt(mean + EPS) * gain_row
            normed[pl.ds(pl.multiple_of(start + i * 64, 64), 64), :] = y.astype(bf16)

        loop(ref.shape[0] // 64, norm)
        start += ref.shape[0]


def weight_copies(gathered_weights, weights, sems):
    ys, xs, zs, rows, _ = gathered_weights.shape
    copies = []
    for y in range(ys):
        for z in range(zs):
            copies.append(
                pltpu.make_async_copy(
                    gathered_weights.at[y, :, z], weights.at[y * zs + z], sems.at[y * zs + z]
                )
            )
    return copies


def attend_half(edge, normed, weights, scale, query, keys, values, put):
    ext, width = normed.shape
    nodes = ext - 2 * HALF
    mine = scale.shape[1]
    heads_of = lambda axis: lax.broadcasted_iota(jnp.int32, (256, 256), axis) // 64
    same_head = (heads_of(0) == heads_of(1)).astype(bf16)

    def unit(y):
        high, low = halves(y * y)
        total = dot(high, same_head) + dot(low, same_head)
        return y * lax.rsqrt(total + EPS)

    flat = weights.reshape(width, weights.shape[-1])

    def project(c):
        start = pl.multiple_of(c * 256, 256)
        cols = pl.ds(start, 256)
        key_cols = pl.ds(pl.multiple_of(mine + start, 256), 256)
        value_cols = pl.ds(pl.multiple_of(2 * mine + start, 256), 256)
        for r in range(nodes // 256):
            rows = pl.ds(r * 256, 256)
            y = dot(normed[pl.ds(HALF + r * 256, 256), :], flat[:, cols])
            query[rows, cols] = (unit(y) * scale[:, cols]).astype(bf16)
        for r in range(ext // 256):
            rows = pl.ds(r * 256, 256)
            keys[rows, cols] = unit(dot(normed[rows, :], flat[:, key_cols])).astype(bf16)
            values[rows, cols] = dot(normed[rows, :], flat[:, value_cols]).astype(bf16)

    loop(mine // 256, project)

    row = lax.broadcasted_iota(jnp.int32, (2 * BLOCK, BLOCK), 0) % BLOCK
    col = lax.broadcasted_iota(jnp.int32, (2 * BLOCK, BLOCK), 1)
    lead = jnp.where(col >= row, 0.0, LOW).astype(f32)
    tail = jnp.where(col < row, 0.0, LOW).astype(f32)
    first_head = lax.broadcasted_iota(jnp.int32, (BLOCK, LANES), 1) < 64
    ones = jnp.ones((2 * HALF + BLOCK, LANES), bf16)
    segments = 2 * HALF // BLOCK + 1
    blocks = nodes // BLOCK
    out_low = jnp.where(edge[0] == 0, LOW, 0.0).astype(f32)
    out_high = jnp.where(edge[0] == edge[1] - 1, LOW, 0.0).astype(f32)

    def attend(p):
        cols = pl.ds(pl.multiple_of(p * LANES, LANES), LANES)
        for b in range(blocks):
            rows = pl.ds(b * BLOCK, BLOCK)
            window = pl.ds(b * BLOCK, 2 * HALF + BLOCK)
            q = query[rows, cols]
            zero = jnp.zeros_like(q)
            pair = jnp.concatenate([jnp.where(first_head, q, zero), jnp.where(first_head, zero, q)], 0)
            score = dot_t(pair, keys[window, cols])
            parts = []
            for s in range(segments):
                part = score[:, s * BLOCK : (s + 1) * BLOCK]
                if s == 0:
                    part = part + lead
                if s == segments - 1:
                    part = part + tail
                if (b + s + 1) * BLOCK <= HALF:
                    part = part + out_low
                if (b + s) * BLOCK >= HALF + nodes:
                    part = part + out_high
                parts.append(part)
            top = functools.reduce(jnp.maximum, parts)
            top = jnp.max(top, -1, keepdims=True)
            weight = jnp.concatenate([jnp.exp(part - top).astype(bf16) for part in parts], 1)
            mixed = dot(weight, jnp.concatenate([values[window, cols], ones], 1))
            mixed = mixed[:, :LANES] / mixed[:, LANES:]
            put(rows, cols, jnp.where(first_head, mixed[:BLOCK], mixed[BLOCK:]).astype(bf16))

    loop(mine // LANES, attend)


def first_kernel(
    edge, before, feats, after, gain, gathered_weights, scale,
    attended, normed,
    weights, query, keys, values, sems,
):
    mine = scale.shape[1]
    copies = weight_copies(gathered_weights.at[..., pl.ds(0, 3 * mine)], weights, sems)
    for copy in copies:
        copy.start()
    normalise(before, feats, after, gain, normed)
    for copy in copies:
        copy.wait()

    def put(rows, cols, value):
        attended[rows, cols] = value

    attend_half(edge, normed, weights, scale, query, keys, values, put)


def second_kernel(
    edge, feats, normed, gathered_mine, gathered_other, scale, attended_mine, w_dec,
    hidden_out, fields_out,
    weights, out_mine, out_other, query, keys, values, attended, sems, sems_mine, sems_other,
):
    nodes, width = feats.shape
    mine = scale.shape[1]
    copies = weight_copies(gathered_other.at[..., pl.ds(0, 3 * mine)], weights, sems)
    copies_out = weight_copies(gathered_mine.at[..., pl.ds(3 * mine, mine)], out_mine, sems_mine)
    copies_out += weight_copies(gathered_other.at[..., pl.ds(3 * mine, mine)], out_other, sems_other)
    for copy in copies + copies_out:
        copy.start()
    here = pl.multiple_of(edge[2] * mine, mine)
    there = pl.multiple_of((1 - edge[2]) * mine, mine)
    attended[:, pl.ds(here, mine)] = attended_mine[...]
    for copy in copies:
        copy.wait()

    def put(rows, cols, value):
        attended[rows, pl.ds(pl.multiple_of(there + cols.start, LANES), LANES)] = value

    attend_half(edge, normed, weights, scale, query, keys, values, put)
    for copy in copies_out:
        copy.wait()
    for half, start in ((out_mine, here), (out_other, there)):
        flat = half.reshape(width, mine)

        def finish(r, flat=flat, start=start):
            rows = pl.ds(pl.multiple_of(r * 256, 256), 256)
            cols = pl.ds(start, mine)
            hidden = feats[rows, cols].astype(f32) + dot(attended[rows, :], flat[...])
            hidden_out[rows, cols] = hidden.astype(bf16)

        loop(nodes // 256, finish)
    fields_out[...] = dot_t(w_dec[...], hidden_out[...]).astype(bf16)


def score_kernel(
    own, same_core, other_core, hidden, targets, cell_node, cell_area,
    score_out, grad_out,
):
    members = 2 * same_core.shape[0]
    nodes = own.shape[1]
    variables, cells = targets.shape
    mine = own[...].astype(f32)
    spread = jnp.zeros_like(mine) - SMOOTH_SQ**0.5
    slope = jnp.zeros_like(mine)
    for ref in (same_core, other_core):
        for j in range(members // 2):
            delta = mine - ref[j].astype(f32)
            square = delta * delta + SMOOTH_SQ
            inverse = lax.rsqrt(square)
            spread = spread + square * inverse
            slope = slope + delta * inverse
    kappa = ALPHA / (2.0 * members * (members - 1)) + (1.0 - ALPHA) / (2.0 * members * members)
    index = lax.broadcasted_iota(jnp.int32, (nodes, cells), 0)
    one_hot = (index == cell_node[...]).astype(bf16)
    high, low = halves(spread)
    fields = dot(own[...], one_hot)
    spread = dot(high, one_hot) + dot(low, one_hot)
    error = fields - targets[...].astype(f32)
    square = error * error + SMOOTH_SQ
    inverse = lax.rsqrt(square)
    score_out[...] = square * inverse * (1.0 / members) - kappa * spread
    area = cell_area[...]
    high, low = halves(area * (error * inverse) * (1.0 / members))
    area_high, area_low = halves(jnp.broadcast_to(area, (8, cells)))
    node_grad = dot_t(high, one_hot) + dot_t(low, one_hot)
    node_area = dot_t(area_high, one_hot) + dot_t(area_low, one_hot)
    node_grad = node_grad - (2.0 * kappa) * slope * node_area[:1]
    grad = dot(node_grad.astype(bf16), hidden[...])
    tiles = grad.shape[1] // LANES
    grad = jnp.concatenate([grad, jnp.zeros((128 - variables, grad.shape[1]), f32)], 0)
    for r in range(128 // 8):
        for c in range(tiles):
            tile = r * tiles + c
            grad_out[tile // 2, pl.ds(tile % 2 * 8, 8), :] = grad[r * 8 : r * 8 + 8, c * LANES : (c + 1) * LANES]


def shifted(value, axis, steps):
    count = lax.axis_size(axis)
    return lax.ppermute(value, axis, [(i, (i + steps) % count) for i in range(count)])


def gathered(x, axis):
    count = lax.axis_size(axis)
    return lax.all_to_all(jnp.broadcast_to(x[None], (count,) + x.shape), axis, 0, 0)


def total(pieces):
    piece = jnp.sum(lax.all_to_all(pieces, GRID, 0, 0), 0)
    piece = jnp.sum(gathered(piece, MEMBER), 0)
    return gathered(piece, GRID)


def body(
    node_feats, norm_gain, w_query, w_key, w_value, w_out, head_scale, w_dec, targets, cell_node, cell_area
):
    feats = node_feats[0]
    nodes, width = feats.shape
    ext = nodes + 2 * HALF
    shards = lax.axis_size(GRID)
    core = lax.axis_index("core")
    variables = w_dec.shape[0]
    up = [(i, i + 1) for i in range(shards - 1)]
    before = lax.ppermute(feats[nodes - HALF :], GRID, up)
    after = lax.ppermute(feats[:HALF], GRID, [(j, i) for i, j in up])

    mine = width // 2
    parts = [
        lax.dynamic_slice_in_dim(w, core * mine, mine, 1) for w in (w_query, w_key, w_value, w_out)
    ]
    shard = jnp.concatenate(parts, 1)
    rows, columns = shard.shape
    lines = lax.axis_size("z_lo")
    lane = gathered(shard, "z_lo")
    whole = gathered(lane, ("y", "x"))
    whole = whole.reshape(lax.axis_size("y"), lax.axis_size("x"), lines, rows, columns)
    other = shifted(whole, "core", 1)

    scale = jnp.repeat(head_scale, width // head_scale.shape[0])[None]
    scale_mine = lax.dynamic_slice_in_dim(scale, core * mine, mine, 1)
    scale_other = lax.dynamic_slice_in_dim(scale, (1 - core) * mine, mine, 1)
    edge = jnp.stack([lax.axis_index(GRID), jnp.int32(shards), core]).astype(jnp.int32)
    smem = pl.BlockSpec(memory_space=pltpu.SMEM)
    vmem = pl.BlockSpec(memory_space=pltpu.VMEM)
    anywhere = pl.BlockSpec(memory_space=pl.ANY)
    params = pltpu.CompilerParams(vmem_limit_bytes=48 * MIB)
    groups = shards // lax.axis_size("x")
    weights = lambda n: pltpu.VMEM((groups, shards // groups, rows, n), bf16)
    heads = [pltpu.VMEM((n, mine), bf16) for n in (nodes, ext, ext)]
    attended, normed = pl.pallas_call(
        first_kernel,
        out_shape=(
            jax.ShapeDtypeStruct((nodes, mine), bf16),
            jax.ShapeDtypeStruct((ext, width), bf16),
        ),
        in_specs=[smem] + [vmem] * 4 + [anywhere, vmem],
        out_specs=(vmem, vmem),
        scratch_shapes=[weights(3 * mine), *heads, pltpu.SemaphoreType.DMA((groups,))],
        compiler_params=params,
        cost_estimate=pl.CostEstimate(flops=8_000_000_000, bytes_accessed=8_000_000, transcendentals=0),
        name="first_heads",
    )(edge, before, feats, after, norm_gain[None], whole, scale_mine)
    hidden, fields = pl.pallas_call(
        second_kernel,
        out_shape=(
            jax.ShapeDtypeStruct((nodes, width), bf16),
            jax.ShapeDtypeStruct((variables, nodes), bf16),
        ),
        in_specs=[smem, vmem, vmem, anywhere, anywhere, vmem, vmem, vmem],
        out_specs=(vmem, vmem),
        scratch_shapes=[
            weights(3 * mine),
            weights(mine),
            weights(mine),
            *heads,
            pltpu.VMEM((nodes, width), bf16),
            pltpu.SemaphoreType.DMA((groups,)),
            pltpu.SemaphoreType.DMA((groups,)),
            pltpu.SemaphoreType.DMA((groups,)),
        ],
        compiler_params=params,
        name="second_heads",
    )(edge, feats, normed, whole, other, scale_other, attended, w_dec)

    same_core = gathered(fields, "z_hi")
    other_core = shifted(same_core, "core", 1)
    score, pieces = pl.pallas_call(
        score_kernel,
        out_shape=(
            jax.ShapeDtypeStruct(targets.shape, f32),
            jax.ShapeDtypeStruct((shards, 16, LANES), f32),
        ),
        in_specs=[vmem] * 7,
        out_specs=(vmem, vmem),
        compiler_params=params,
        name="score",
    )(fields, same_core, other_core, hidden, targets, cell_node[None], cell_area[None])
    grad = total(pieces).reshape(16, width // LANES, 8, LANES).transpose(0, 2, 1, 3)
    return score[None], grad.reshape(128, width)[:variables]


def solution(mesh):
    fine = Mesh(mesh.devices.reshape(4, 2, 4, 4, 4), MEMBER + GRID)
    in_specs = (
        P(MEMBER, GRID, None),
        P(),
        P(GRID, None),
        P(GRID, None),
        P(GRID, None),
        P(GRID, None),
        P(),
        P(),
        P(None, GRID),
        P(GRID),
        P(GRID),
    )
    out_specs = (P(MEMBER, None, GRID), P())
    return jax.shard_map(body, mesh=fine, in_specs=in_specs, out_specs=out_specs, check_vma=False)
```

time: 2010 us -> 241 us (0.12)
  waiting for transfers between devices: 1780 us -> 27.8 us
  blocking collectives: 0 us -> 140 us
  starting transfers between devices: 107 us -> 32.5 us
  matrix products: 64.7 us -> 0 us
  Pallas kernels: 0 us -> 34.1 us
  local copies, waits for them, and re-layouts: 27 us -> 5.1 us
    all_gather x4 -> x0, waiting for transfers between devices: 1290 us -> none  [the longest x1 350 us: body(): lax.all_gather(w_value, 'grid', axis=0, tiled=True)]
    psum x1 -> x0, waiting for transfers between devices: 455 us -> none  [body(): grad_dec = lax.psum(local_grad, ('member', 'grid'))]
    all_to_all x0 -> x5, blocking collectives: none -> 140 us  [the longest x4 114 us: gathered(): lax.all_to_all(jnp.broadcast_to(x[None], (count,) + x.shape), axis, 0, 0)]
    ppermute x9 -> x4, starting transfers between devices: 107 us -> 27.5 us  [the longest x2 22.2 us: shifted(): lax.ppermute(value, axis, [(i, (i + steps) % count) for i in range(count)])]
    dot_general x11 -> x0, matrix products: 36.3 us -> none  [the longest x4 20.1 us: attend(): jnp.einsum('hne,ehd->nhd', weights, values_grp, preferred_element_type=jn...]
    pallas_call x0 -> x3, Pallas kernels: none -> 34.1 us  [the longest x1 16.9 us: body(): pl.pallas_call(second_kernel, out_shape=(jax.ShapeDtypeStruct((nodes, wid...]
    sub x4 -> x0, matrix products: 28.4 us -> none  [attend(): expo = jnp.exp(score - top)]
    ppermute x9 -> x4, waiting for transfers between devices: 33.5 us -> 11.9 us  [the longest x1 9.83 us: body(): after = lax.ppermute(feats[:HALF], GRID, [(j, i) for i, j in up])]
  transfers between devices with their start and end apart: 14 -> 5, of which waited for: 12 -> 4; matrix products, arithmetic and copies ran while one was open for 4% -> 1% of each run, Pallas kernels for 0% -> 6%
where the time goes in v1:
time: 241 us; the launch traced here: 240 us
  blocking collectives  140 us (58%)
  Pallas kernels  34.1 us (14%)
  starting transfers between devices  32.5 us (13%)
  waiting for transfers between devices  27.8 us (12%)
  local copies, waits for them, and re-layouts  5.1 us (2%)
    all_to_all x4, blocking collectives, gathered(): lax.all_to_all(jnp.broadcast_to(x[None], (count,) + x.shape), axis, 0, 0)  114 us
    all_to_all x1, blocking collectives, total(): piece = jnp.sum(lax.all_to_all(pieces, GRID, 0, 0), 0)  25.4 us
    ppermute x2, starting transfers between devices, shifted(): lax.ppermute(value, axis, [(i, (i + steps) % count) for i in range(count)])  22.2 us
    pallas_call x1, Pallas kernels, body(): pl.pallas_call(second_kernel, out_shape=(jax.ShapeDtypeStruct((nodes, wid...  16.9 us
    all_to_all x1, waiting for transfers between devices, gathered(): lax.all_to_all(jnp.broadcast_to(x[None], (count,) + x.shape), axis, 0, 0)  15.9 us
    pallas_call x1, Pallas kernels, body(): pl.pallas_call(first_kernel, out_shape=(jax.ShapeDtypeStruct((nodes, mine...  14.5 us
    ppermute x1, waiting for transfers between devices, body(): after = lax.ppermute(feats[:HALF], GRID, [(j, i) for i, j in up])  9.83 us
    all_to_all x1, starting transfers between devices, gathered(): lax.all_to_all(jnp.broadcast_to(x[None], (count,) + x.shape), axis, 0, 0)  5.05 us
  transfers between devices with their start and end apart: 5, of which 4 were waited for; matrix products, arithmetic and copies ran while one was open for 1% of the time, Pallas kernels for 6%

profile of v1, /device:TPU:1, one launch (start us, length us, event | category | flops | bytes accessed | tf_op | source)
XLA Modules:
  0.0 240.2 jit_solution(15757357689708634692)
XLA Ops:
  0.6 0.7 constant_dynamic-slice_fusion.4
  1.4 0.7 constant_dynamic-slice_fusion.2
  2.2 12.2 %all_to_all.30 = bf16[4,16,2048]{2,1,0:T(8,128)(2,1)S(1)} all-to-all(bf16[4,16,2048]{2,1,0:T(8,128)(2,1)S(1)} %broadcast_in_dim.21), channel_id=1, replica_groups=mesh['z_hi'=4,'core'=2,'y'=4,'z_lo'=4,'x'=4] {'z_lo'}, dimensions={0} | all-to-all | bytes 524288 | tf_op jit(solution)/shard_map/all_to_all | solution.py:252
  14.4 0.5 broadcast_in_dim.22
  14.9 55.5 %all_to_all.31 = bf16[16,4,16,2048]{3,2,1,0:T(8,128)(2,1)} all-to-all(bf16[16,4,16,2048]{3,2,1,0:T(8,128)(2,1)S(1)} %broadcast_in_dim.22), channel_id=1, replica_groups=mesh['z_hi'=4,'core'=2,'y'=4,'z_lo'=4,'x'=4] {'y','x'}, dimensions={0} | all-to-all | bytes 8388608 | tf_op jit(solution)/shard_map/all_to_all | solution.py:252
  70.4 6.3 %collective-permute-start.2 = (bf16[4,4,4,16,2048]{4,3,2,1,0:T(8,128)(2,1)}, bf16[4,4,4,16,2048]{4,3,2,1,0:T(8,128)(2,1)}, u32[]{:S(2)}, u32[]{:S(2)}) collective-permute-start(bf16[4,4,4,16,2048]{4,3,2,1,0:T(8,128)(2,1)} %bitcast.5.gathered_weights.gathered_mine), channel_id=1, source_target_pairs={{0,64},{64,0},{1,65},{65,1},{2,66},{66,2},{3,67},{67,3},{4,68},{68... | collective-permute-start | bytes 12582920 | tf_op jit(solution)/shard_map/ppermute | solution.py:247
  76.8 1.3 collective-permute-start.1
  78.1 4.0 %collective-permute-start = (bf16[256,1024]{1,0:T(8,128)(2,1)S(1)}, bf16[256,1024]{1,0:T(8,128)(2,1)S(1)}, u32[]{:S(2)}, u32[]{:S(2)}) collective-permute-start(bf16[256,1024]{1,0:T(8,128)(2,1)S(1)} %get-tuple-element.19), channel_id=1, source_target_pairs={{0,1},{1,2},{2,3},{3,4},{4,5},{5,6},{6,7},{7,8},{8,9},{9,10},{10,1... | collective-permute-start | bytes 1572872 | tf_op jit(solution)/shard_map/ppermute | solution.py:271
  82.2 0.1 broadcast_in_dim_reshape.3
  82.4 9.8 %collective-permute-done.1.after = bf16[256,1024]{1,0:T(8,128)(2,1)S(1)} collective-permute-done((bf16[256,1024]{1,0:T(8,128)(2,1)S(1)}, bf16[256,1024]{1,0:T(8,128)(2,1)S(1)}, u32[]{:S(2)}, u32[]{:S(2)}) %collective-permute-start.1) | collective-permute-done | bytes 524320 | tf_op jit(solution)/shard_map/ppermute | solution.py:272
  92.2 0.9 collective-permute-done.before
  93.1 14.5 %first_heads.1 = (bf16[512,512]{1,0:T(8,128)(2,1)S(1)}, bf16[1024,1024]{1,0:T(8,128)(2,1)S(1)}) custom-call(s32[3]{0:T(128)S(1)} %pad_add_fusion.edge, bf16[256,1024]{1,0:T(8,128)(2,1)S(1)} %collective-permute-done.before, bf16[512,1024]{1,0:T(8,128)(2,1)S(1)} %bitcast.16, bf16[256,1024]{1,0:T(8,128)(2,1)S(1)} %collective-permute-done.1.after, ...), custom_call_target="tpu_custom_call" | custom-call | flops 8000000000 | bytes 8000000 | tf_op jit(solution)/shard_map/first_heads/pallas_call | solution.py:297
  107.6 16.9 %second_heads.1 = (bf16[512,1024]{1,0:T(8,128)(2,1)S(1)}, bf16[100,512]{1,0:T(8,128)(2,1)S(1)}) custom-call(s32[3]{0:T(128)S(1)} %pad_add_fusion.edge, bf16[512,1024]{1,0:T(8,128)(2,1)S(1)} %bitcast.17, bf16[1024,1024]{1,0:T(8,128)(2,1)S(1)} %get-tuple-element.8.normed, bf16[4,4,4,16,2048]{4,3,2,1,0:T(8,128)(2,1)} %bitcast.5.gathered_weights.gathered_mine, ...), custom_call_target="tpu_custom_call" | custom-call | tf_op jit(solution)/shard_map/second_heads/pallas_call | solution.py:310
  124.6 27.5 %all_to_all.32.same_core = bf16[4,100,512]{2,1,0:T(8,128)(2,1)S(1)} all-to-all(bf16[4,100,512]{2,1,0:T(8,128)(2,1)S(1)} %broadcast_in_dim.24), channel_id=1, replica_groups=mesh['z_hi'=4,'core'=2,'y'=4,'z_lo'=4,'x'=4] {'z_hi'}, dimensions={0} | all-to-all | bytes 819200 | tf_op jit(solution)/shard_map/all_to_all | solution.py:252
  152.1 15.9 %collective-permute-start.3 = (bf16[4,100,512]{2,1,0:T(8,128)(2,1)S(1)}, bf16[4,100,512]{2,1,0:T(8,128)(2,1)S(1)}, u32[]{:S(2)}, u32[]{:S(2)}) collective-permute-start(bf16[4,100,512]{2,1,0:T(8,128)(2,1)S(1)} %all_to_all.32.same_core), channel_id=1, source_target_pairs={{0,64},{64,0},{1,65},{65,1},{2,66},{66,2},{3,67},{67,3},{4,68},{68... | collective-permute-start | bytes 1228808 | tf_op jit(solution)/shard_map/ppermute | solution.py:247
  168.0 1.2 collective-permute-done.3.other_core
  169.2 2.7 %score.1 = (f32[100,1024]{1,0:T(8,128)S(1)}, f32[64,16,128]{2,1,0:T(8,128)S(1)}) custom-call(bf16[100,512]{1,0:T(8,128)(2,1)S(1)} %get-tuple-element.10.own, bf16[4,100,512]{2,1,0:T(8,128)(2,1)S(1)} %all_to_all.32.same_core, bf16[4,100,512]{2,1,0:T(8,128)(2,1)S(1)} %collective-permute-done.3.other_core, bf16[512,1024]{1,0:T(8,128)(2,1)S(1)} %get-tuple-element.11.hidden, ...), custom_call_target="tpu_custom_call" | custom-call | tf_op jit(solution)/shard_map/score/pallas_call | solution.py:334
  171.9 25.4 %all_to_all.33 = f32[64,16,128]{2,1,0:T(8,128)S(1)} all-to-all(f32[64,16,128]{2,1,0:T(8,128)S(1)} %get-tuple-element.13), channel_id=1, replica_groups=mesh['z_hi'=4,'core'=2,'y'=4,'z_lo'=4,'x'=4] {'y','z_lo','x'}, dimensions={0} | all-to-all | bytes 1048576 | tf_op jit(solution)/shard_map/all_to_all | solution.py:256
  197.4 19.0 %all_to_all.34 = f32[8,16,128]{2,1,0:T(8,128)S(1)} all-to-all(f32[8,16,128]{2,1,0:T(8,128)S(1)} %broadcast_in_dim.53), channel_id=1, replica_groups=mesh['z_hi'=4,'core'=2,'y'=4,'z_lo'=4,'x'=4] {'z_hi','core'}, dimensions={0} | all-to-all | bytes 131072 | tf_op jit(solution)/shard_map/all_to_all | solution.py:252
  216.4 0.8 broadcast_in_dim.54
  217.2 5.1 %all-to-all-start.5 = ((f32[64,16,128]{2,1,0:T(8,128)}), f32[64,16,128]{2,1,0:T(8,128)S(1)}, u32[]{:S(2)}, u32[]{:S(2)}) async-start(f32[64,16,128]{2,1,0:T(8,128)} %broadcast_in_dim.54), calls=%async_computation.5 | async-start | bytes 1048576 | tf_op jit(solution)/shard_map/all_to_all | solution.py:252
  222.2 1.2 copy.14
  223.4 15.9 %all-to-all-done.5 = f32[64,16,128]{2,1,0:T(8,128)S(1)} async-done(((f32[64,16,128]{2,1,0:T(8,128)}), f32[64,16,128]{2,1,0:T(8,128)S(1)}, u32[]{:S(2)}, u32[]{:S(2)}) %all-to-all-start.5) | async-done | bytes 524320 | tf_op jit(solution)/shard_map/all_to_all | solution.py:252
  239.4 0.8 slice.20
  (26 shorter events, 0.4 us)
Async XLA Ops:
  14.9 61.8 %copy-start = (bf16[1,512,1024]{2,1,0:T(8,128)(2,1)S(1)}, bf16[1,512,1024]{2,1,0:T(8,128)(2,1)}, u32[]{:S(2)}) copy-start(bf16[1,512,1024]{2,1,0:T(8,128)(2,1)} %param.11) | copy-start | bytes 3145732
  14.9 67.2 %copy-start.5 = (bf16[1024]{0:T(1024)(128)(2,1)S(1)}, bf16[1024]{0:T(1024)(128)(2,1)}, u32[]{:S(2)}) copy-start(bf16[1024]{0:T(1024)(128)(2,1)} %param.12) | copy-start | bytes 6148
  14.9 67.2 %copy-start.6 = (f32[16]{0:T(128)S(1)}, f32[16]{0:T(128)}, u32[]{:S(2)}) copy-start(f32[16]{0:T(128)} %param.17) | copy-start | bytes 196
  70.4 37.2 %collective-permute-start.2 = (bf16[4,4,4,16,2048]{4,3,2,1,0:T(8,128)(2,1)}, bf16[4,4,4,16,2048]{4,3,2,1,0:T(8,128)(2,1)}, u32[]{:S(2)}, u32[]{:S(2)}) collective-permute-start(bf16[4,4,4,16,2048]{4,3,2,1,0:T(8,128)(2,1)} %bitcast.5.gathered_weights.gathered_mine), channel_id=1, source_target_pairs={{0,64},{64,0},{1,65},{65,1},{2,66},{66,2},{3,67},{67,3},{4,68},{68... | collective-permute-start | bytes 12582920 | tf_op jit(solution)/shard_map/ppermute | solution.py:247
  76.8 15.4 %collective-permute-start.1 = (bf16[256,1024]{1,0:T(8,128)(2,1)S(1)}, bf16[256,1024]{1,0:T(8,128)(2,1)S(1)}, u32[]{:S(2)}, u32[]{:S(2)}) collective-permute-start(bf16[256,1024]{1,0:T(8,128)(2,1)S(1)} %get-tuple-element.18), channel_id=1, source_target_pairs={{1,0},{2,1},{3,2},{4,3},{5,4},{6,5},{7,6},{8,7},{9,8},{10,9},{11,1... | collective-permute-start | bytes 1572872 | tf_op jit(solution)/shard_map/ppermute | solution.py:272
  78.1 15.0 %collective-permute-start = (bf16[256,1024]{1,0:T(8,128)(2,1)S(1)}, bf16[256,1024]{1,0:T(8,128)(2,1)S(1)}, u32[]{:S(2)}, u32[]{:S(2)}) collective-permute-start(bf16[256,1024]{1,0:T(8,128)(2,1)S(1)} %get-tuple-element.19), channel_id=1, source_target_pairs={{0,1},{1,2},{2,3},{3,4},{4,5},{5,6},{6,7},{7,8},{8,9},{9,10},{10,1... | collective-permute-start | bytes 1572872 | tf_op jit(solution)/shard_map/ppermute | solution.py:271
  93.1 14.5 %copy-start.2 = (bf16[100,1024]{1,0:T(8,128)(2,1)S(1)}, bf16[100,1024]{1,0:T(8,128)(2,1)}, u32[]{:S(2)}) copy-start(bf16[100,1024]{1,0:T(8,128)(2,1)} %w_dec.1) | copy-start | bytes 614404
  107.6 61.6 %copy-start.1 = (bf16[100,1024]{1,0:T(8,128)(2,1)S(1)}, bf16[100,1024]{1,0:T(8,128)(2,1)}, u32[]{:S(2)}) copy-start(bf16[100,1024]{1,0:T(8,128)(2,1)} %targets.1) | copy-start | bytes 614404
  107.6 61.6 %copy-start.3 = (s32[1024]{0:T(1024)S(1)}, s32[1024]{0:T(1024)}, u32[]{:S(2)}) copy-start(s32[1024]{0:T(1024)} %param.20) | copy-start | bytes 12292
  107.6 61.6 %copy-start.4 = (f32[1024]{0:T(1024)S(1)}, f32[1024]{0:T(1024)}, u32[]{:S(2)}) copy-start(f32[1024]{0:T(1024)} %param.21) | copy-start | bytes 12292
  152.1 17.1 %collective-permute-start.3 = (bf16[4,100,512]{2,1,0:T(8,128)(2,1)S(1)}, bf16[4,100,512]{2,1,0:T(8,128)(2,1)S(1)}, u32[]{:S(2)}, u32[]{:S(2)}) collective-permute-start(bf16[4,100,512]{2,1,0:T(8,128)(2,1)S(1)} %all_to_all.32.same_core), channel_id=1, source_target_pairs={{0,64},{64,0},{1,65},{65,1},{2,66},{66,2},{3,67},{67,3},{4,68},{68... | collective-permute-start | bytes 1228808 | tf_op jit(solution)/shard_map/ppermute | solution.py:247
  217.2 22.2 %all-to-all-start.5 = ((f32[64,16,128]{2,1,0:T(8,128)}), f32[64,16,128]{2,1,0:T(8,128)S(1)}, u32[]{:S(2)}, u32[]{:S(2)}) async-start(f32[64,16,128]{2,1,0:T(8,128)} %broadcast_in_dim.54), calls=%async_computation.5 | async-start | bytes 1048576 | tf_op jit(solution)/shard_map/all_to_all | solution.py:252

commit v2 on v1

v2 whole, which is shorter than its diff:
```python
import functools

import jax
import jax.numpy as jnp
from jax import lax
from jax.experimental import pallas as pl
from jax.experimental.pallas import tpu as pltpu
from jax.sharding import Mesh, PartitionSpec as P

HALF = 256
EPS = 1e-06
SMOOTH_SQ = 0.0625
ALPHA = 0.95
LANES = 128
BLOCK = 128
LOW = -1e30
MIB = 1024 * 1024

GRID = ("y", "z_lo", "x")
MEMBER = ("z_hi", "core")
PLANE = ("core", "y", "x")
LINE = ("z_hi", "z_lo")

f32 = jnp.float32
bf16 = jnp.bfloat16


def dot(a, b):
    return jnp.dot(a, b, preferred_element_type=f32)


def dot_t(a, b):
    return lax.dot_general(a, b, (((1,), (1,)), ((), ())), preferred_element_type=f32)


def halves(x):
    high = x.astype(bf16)
    return high, (x - high.astype(f32)).astype(bf16)


def loop(count, fn):
    def step(i, _):
        fn(i)
        return 0

    lax.fori_loop(0, count, step, 0)


def normalise(before, feats, after, gain, normed):
    gain_row = gain[...].astype(f32)
    start = 0
    for ref in (before, feats, after):

        def norm(i, ref=ref, start=start):
            x = ref[pl.ds(pl.multiple_of(i * 64, 64), 64), :].astype(f32)
            mean = jnp.mean(x * x, -1, keepdims=True)
            y = x * lax.rsqrt(mean + EPS) * gain_row
            normed[pl.ds(pl.multiple_of(start + i * 64, 64), 64), :] = y.astype(bf16)

        loop(ref.shape[0] // 64, norm)
        start += ref.shape[0]


def weight_copies(gathered_weights, weights, sems):
    ys, xs, zs, rows, _ = gathered_weights.shape
    copies = []
    for y in range(ys):
        for z in range(zs):
            copies.append(
                pltpu.make_async_copy(
                    gathered_weights.at[y, :, z], weights.at[y * zs + z], sems.at[y * zs + z]
                )
            )
    return copies


def attend_pairs(edge, normed, weights, scale, base, query, keys, values, attended):
    ext, width = normed.shape
    nodes = ext - 2 * HALF
    pairs = weights.shape[-1] // (3 * LANES)
    flat = weights.reshape(width, weights.shape[-1])

    def unit(y):
        first_head = lax.broadcasted_iota(jnp.int32, y.shape, 1) < 64
        square = y * y
        first = jnp.sum(jnp.where(first_head, square, 0.0), -1, keepdims=True)
        second = jnp.sum(jnp.where(first_head, 0.0, square), -1, keepdims=True)
        return y * lax.rsqrt(jnp.where(first_head, first, second) + EPS)

    for p in range(pairs):
        cols = pl.ds(p * LANES, LANES)
        query_cols = pl.ds(p * 3 * LANES, LANES)
        keyval_cols = pl.ds(p * 3 * LANES + LANES, 2 * LANES)
        factor = scale[:, pl.ds(pl.multiple_of(base + p * LANES, LANES), LANES)]
        for r in range(nodes // 256):
            rows = pl.ds(r * 256, 256)
            y = dot(normed[pl.ds(HALF + r * 256, 256), :], flat[:, query_cols])
            query[rows, cols] = (unit(y) * factor).astype(bf16)
        for r in range(ext // 256):
            rows = pl.ds(r * 256, 256)
            y = dot(normed[rows, :], flat[:, keyval_cols])
            keys[rows, cols] = unit(y[:, :LANES]).astype(bf16)
            values[rows, cols] = y[:, LANES:].astype(bf16)

    row = lax.broadcasted_iota(jnp.int32, (2 * BLOCK, BLOCK), 0) % BLOCK
    col = lax.broadcasted_iota(jnp.int32, (2 * BLOCK, BLOCK), 1)
    lead = jnp.where(col >= row, 0.0, LOW).astype(f32)
    tail = jnp.where(col < row, 0.0, LOW).astype(f32)
    first_head = lax.broadcasted_iota(jnp.int32, (BLOCK, LANES), 1) < 64
    ones = jnp.ones((2 * HALF + BLOCK, LANES), bf16)
    segments = 2 * HALF // BLOCK + 1
    out_low = jnp.where(edge[0] == 0, LOW, 0.0).astype(f32)
    out_high = jnp.where(edge[0] == edge[1] - 1, LOW, 0.0).astype(f32)
    for p in range(pairs):
        cols = pl.ds(p * LANES, LANES)
        for b in range(nodes // BLOCK):
            rows = pl.ds(b * BLOCK, BLOCK)
            window = pl.ds(b * BLOCK, 2 * HALF + BLOCK)
            q = query[rows, cols]
            zero = jnp.zeros_like(q)
            pair = jnp.concatenate([jnp.where(first_head, q, zero), jnp.where(first_head, zero, q)], 0)
            score = dot_t(pair, keys[window, cols])
            parts = []
            for s in range(segments):
                part = score[:, s * BLOCK : (s + 1) * BLOCK]
                if s == 0:
                    part = part + lead
                if s == segments - 1:
                    part = part + tail
                if (b + s + 1) * BLOCK <= HALF:
                    part = part + out_low
                if (b + s) * BLOCK >= HALF + nodes:
                    part = part + out_high
                parts.append(part)
            top = functools.reduce(jnp.maximum, parts)
            top = jnp.max(top, -1, keepdims=True)
            weight = jnp.concatenate([jnp.exp(part - top).astype(bf16) for part in parts], 1)
            mixed = dot(weight, jnp.concatenate([values[window, cols], ones], 1))
            mixed = mixed[:, :LANES] / mixed[:, LANES:]
            attended[rows, cols] = jnp.where(first_head, mixed[:BLOCK], mixed[BLOCK:]).astype(bf16)


def mine_kernel(
    edge, before, feats, after, gain, gathered_weights, scale,
    attended, normed,
    weights, query, keys, values, sems,
):
    copies = weight_copies(gathered_weights, weights, sems)
    for copy in copies:
        copy.start()
    normalise(before, feats, after, gain, normed)
    for copy in copies:
        copy.wait()
    base = edge[2] * (scale.shape[1] // 2)
    attend_pairs(edge, normed, weights, scale, base, query, keys, values, attended)


def other_kernel(
    edge, normed, gathered_weights, scale,
    attended,
    weights, query, keys, values, sems,
):
    copies = weight_copies(gathered_weights, weights, sems)
    for copy in copies:
        copy.start()
    for copy in copies:
        copy.wait()
    base = (1 - edge[2]) * (scale.shape[1] // 2)
    attend_pairs(edge, normed, weights, scale, base, query, keys, values, attended)


def hidden_kernel(
    edge, feats, attended_mine, attended_other, gathered_mine, gathered_other, w_dec,
    hidden_out, fields_out,
    out_mine, out_other, sems_mine, sems_other,
):
    nodes, width = feats.shape
    mine = width // 2
    copies = weight_copies(gathered_mine, out_mine, sems_mine)
    copies += weight_copies(gathered_other, out_other, sems_other)
    for copy in copies:
        copy.start()
    here = pl.ds(pl.multiple_of(edge[2] * mine, mine), mine)
    there = pl.ds(pl.multiple_of((1 - edge[2]) * mine, mine), mine)
    for copy in copies:
        copy.wait()
    for half, cols in ((out_mine, here), (out_other, there)):
        flat = half.reshape(width, mine)
        for r in range(nodes // 256):
            rows = pl.ds(r * 256, 256)
            projected = dot(attended_mine[rows, :], flat[here, :]) + dot(attended_other[rows, :], flat[there, :])
            hidden_out[rows, cols] = (feats[rows, cols].astype(f32) + projected).astype(bf16)
    fields_out[...] = dot_t(w_dec[...], hidden_out[...]).astype(bf16)


def score_kernel(
    own, same_core, other_core, hidden, targets, cell_node, cell_area,
    score_out, grad_out,
):
    members = 2 * same_core.shape[0]
    nodes = own.shape[1]
    variables, cells = targets.shape
    mine = own[...].astype(f32)
    spread = jnp.zeros_like(mine) - SMOOTH_SQ**0.5
    slope = jnp.zeros_like(mine)
    for ref in (same_core, other_core):
        for j in range(members // 2):
            delta = mine - ref[j].astype(f32)
            square = delta * delta + SMOOTH_SQ
            inverse = lax.rsqrt(square)
            spread = spread + square * inverse
            slope = slope + delta * inverse
    kappa = ALPHA / (2.0 * members * (members - 1)) + (1.0 - ALPHA) / (2.0 * members * members)
    index = lax.broadcasted_iota(jnp.int32, (nodes, cells), 0)
    one_hot = (index == cell_node[...]).astype(bf16)
    high, low = halves(spread)
    fields = dot(own[...], one_hot)
    spread = dot(high, one_hot) + dot(low, one_hot)
    error = fields - targets[...].astype(f32)
    square = error * error + SMOOTH_SQ
    inverse = lax.rsqrt(square)
    score_out[...] = square * inverse * (1.0 / members) - kappa * spread
    area = cell_area[...]
    high, low = halves(area * (error * inverse) * (1.0 / members))
    area_high, area_low = halves(jnp.broadcast_to(area, (8, cells)))
    node_grad = dot_t(high, one_hot) + dot_t(low, one_hot)
    node_area = dot_t(area_high, one_hot) + dot_t(area_low, one_hot)
    node_grad = node_grad - (2.0 * kappa) * slope * node_area[:1]
    grad = dot(node_grad.astype(bf16), hidden[...])
    tiles = grad.shape[1] // LANES
    each = grad_out.shape[1] // 16
    grad = jnp.concatenate([grad, jnp.zeros((128 - variables, grad.shape[1]), f32)], 0).astype(bf16)
    for r in range(128 // 16):
        for c in range(tiles):
            tile = r * tiles + c
            grad_out[tile // each, pl.ds(tile % each * 16, 16), :] = grad[
                r * 16 : r * 16 + 16, c * LANES : (c + 1) * LANES
            ]


def shifted(value, axis, steps):
    count = lax.axis_size(axis)
    return lax.ppermute(value, axis, [(i, (i + steps) % count) for i in range(count)])


def gathered(x, axis):
    count = lax.axis_size(axis)
    return lax.all_to_all(jnp.broadcast_to(x[None], (count,) + x.shape), axis, 0, 0)


def total(pieces):
    piece = jnp.sum(lax.all_to_all(pieces, PLANE, 0, 0).astype(f32), 0)
    piece = jnp.sum(gathered(piece.astype(bf16), LINE).astype(f32), 0)
    return gathered(piece.astype(bf16), PLANE).astype(f32)


def body(
    node_feats, norm_gain, w_query, w_key, w_value, w_out, head_scale, w_dec, targets, cell_node, cell_area
):
    feats = node_feats[0]
    nodes, width = feats.shape
    ext = nodes + 2 * HALF
    shards = lax.axis_size(GRID)
    core = lax.axis_index("core")
    variables = w_dec.shape[0]
    up = [(i, i + 1) for i in range(shards - 1)]
    before = lax.ppermute(feats[nodes - HALF :], GRID, up)
    after = lax.ppermute(feats[:HALF], GRID, [(j, i) for i, j in up])

    mine = width // 2
    rows = w_query.shape[0]
    parts = [
        lax.dynamic_slice_in_dim(w, core * mine, mine, 1) for w in (w_query, w_key, w_value, w_out)
    ]
    by_pair = jnp.stack([w.reshape(rows, mine // LANES, LANES) for w in parts[:3]], 2)
    shard = jnp.concatenate([by_pair.reshape(rows, 3 * mine), parts[3]], 1)
    lane = gathered(shard, "z_lo")
    grouped = lambda w: w.reshape((lax.axis_size("y"), lax.axis_size("x")) + w.shape[1:])
    heads_mine = gathered(lane[..., : 3 * mine], ("y", "x"))
    heads_mine, before, after, lane_out = lax.optimization_barrier(
        (heads_mine, before, after, lane[..., 3 * mine :])
    )
    heads_mine = grouped(heads_mine)
    out_mine = grouped(gathered(lane_out, ("y", "x")))
    heads_other = shifted(heads_mine, "core", 1)

    scale = jnp.repeat(head_scale, width // head_scale.shape[0])[None]
    edge = jnp.stack([lax.axis_index(GRID), jnp.int32(shards), core]).astype(jnp.int32)
    smem = pl.BlockSpec(memory_space=pltpu.SMEM)
    vmem = pl.BlockSpec(memory_space=pltpu.VMEM)
    anywhere = pl.BlockSpec(memory_space=pl.ANY)
    params = pltpu.CompilerParams(vmem_limit_bytes=28 * MIB)
    groups = shards // lax.axis_size("x")
    weights = lambda n: pltpu.VMEM((groups, shards // groups, rows, n), bf16)
    sems = pltpu.SemaphoreType.DMA((groups,))
    heads = [pltpu.VMEM((n, mine), bf16) for n in (nodes, ext, ext)]
    cost = pl.CostEstimate(flops=4_000_000_000, bytes_accessed=8_000_000, transcendentals=0)
    half = jax.ShapeDtypeStruct((nodes, mine), bf16)
    attended_mine, normed = pl.pallas_call(
        mine_kernel,
        out_shape=(half, jax.ShapeDtypeStruct((ext, width), bf16)),
        in_specs=[smem] + [vmem] * 4 + [anywhere, vmem],
        out_specs=(vmem, vmem),
        scratch_shapes=[weights(3 * mine), *heads, sems],
        compiler_params=params,
        cost_estimate=cost,
        name="heads_mine",
    )(edge, before, feats, after, norm_gain[None], heads_mine, scale)
    attended_other = pl.pallas_call(
        other_kernel,
        out_shape=half,
        in_specs=[smem, vmem, anywhere, vmem],
        out_specs=vmem,
        scratch_shapes=[weights(3 * mine), *heads, sems],
        compiler_params=params,
        cost_estimate=cost,
        name="heads_other",
    )(edge, normed, heads_other, scale)
    out_mine, attended_mine = lax.optimization_barrier((out_mine, attended_mine))
    out_other = shifted(out_mine, "core", 1)
    hidden, fields = pl.pallas_call(
        hidden_kernel,
        out_shape=(
            jax.ShapeDtypeStruct((nodes, width), bf16),
            jax.ShapeDtypeStruct((variables, nodes), bf16),
        ),
        in_specs=[smem, vmem, vmem, vmem, anywhere, anywhere, vmem],
        out_specs=(vmem, vmem),
        scratch_shapes=[weights(mine), weights(mine), sems, sems],
        compiler_params=params,
        name="hidden",
    )(edge, feats, attended_mine, attended_other, out_mine, out_other, w_dec)

    same_core = gathered(fields, "z_hi")
    other_core = shifted(same_core, "core", 1)
    pieces = lax.axis_size(PLANE)
    score, grad = pl.pallas_call(
        score_kernel,
        out_shape=(
            jax.ShapeDtypeStruct(targets.shape, f32),
            jax.ShapeDtypeStruct((pieces, width // pieces, LANES), bf16),
        ),
        in_specs=[vmem] * 7,
        out_specs=(vmem, vmem),
        compiler_params=params,
        name="score",
    )(fields, same_core, other_core, hidden, targets, cell_node[None], cell_area[None])
    grad = total(grad).reshape(8, width // LANES, 16, LANES).transpose(0, 2, 1, 3)
    return score[None], grad.reshape(128, width)[:variables]


def solution(mesh):
    fine = Mesh(mesh.devices.reshape(4, 2, 4, 4, 4), MEMBER + GRID)
    in_specs = (
        P(MEMBER, GRID, None),
        P(),
        P(GRID, None),
        P(GRID, None),
        P(GRID, None),
        P(GRID, None),
        P(),
        P(),
        P(None, GRID),
        P(GRID),
        P(GRID),
    )
    out_specs = (P(MEMBER, None, GRID), P())
    return jax.shard_map(body, mesh=fine, in_specs=in_specs, out_specs=out_specs, check_vma=False)
```

time: 241 us -> 218 us (0.905)
  blocking collectives: 140 us -> 70.4 us
  waiting for transfers between devices: 27.8 us -> 58.7 us
  starting transfers between devices: 32.5 us -> 46.4 us
  local copies, waits for them, and re-layouts: 5.1 us -> 11.2 us
  Pallas kernels: 34.1 us -> 28.8 us
    all_to_all x4 -> x3, blocking collectives: 114 us -> 58.9 us  [gathered(): lax.all_to_all(jnp.broadcast_to(x[None], (count,) + x.shape), axis, 0, 0)]
    ppermute x1, waiting for transfers between devices: 0.86 us -> 39.9 us  [body(): before = lax.ppermute(feats[nodes - HALF:], GRID, up)]
    all_to_all x1 -> x3, starting transfers between devices: 5.05 us -> 21.2 us  [gathered(): lax.all_to_all(jnp.broadcast_to(x[None], (count,) + x.shape), axis, 0, 0)]
    all_to_all x1, blocking collectives: 25.4 us -> 11.6 us  [total(): piece = jnp.sum(lax.all_to_all(pieces, PLANE, 0, 0).astype(f32), 0)]
    pallas_call x2 -> x3, Pallas kernels: 31.4 us -> 26.1 us  [the longest x1 11.5 us: body(): pl.pallas_call(mine_kernel, out_shape=(half, jax.ShapeDtypeStruct((ext, w...]
    ppermute x1, waiting for transfers between devices: 9.83 us -> 5.22 us  [body(): after = lax.ppermute(feats[:HALF], GRID, [(j, i) for i, j in up])]
    unnamed x15 -> x24, local copies, waits for them, and re-layouts: 1.22 us -> 5.24 us
    all_to_all x1 -> x3, waiting for transfers between devices: 15.9 us -> 12.4 us  [gathered(): lax.all_to_all(jnp.broadcast_to(x[None], (count,) + x.shape), axis, 0, 0)]
  transfers between devices with their start and end apart: 5 -> 8, of which waited for: 4 -> 6; matrix products, arithmetic and copies ran while one was open for 1% -> 1% of each run, Pallas kernels for 6% -> 11%
where the time goes in v2:
time: 218 us
  blocking collectives  70.4 us (32%)
  waiting for transfers between devices  58.7 us (27%)
  starting transfers between devices  46.4 us (21%)
  Pallas kernels  28.8 us (13%)
  local copies, waits for them, and re-layouts  11.2 us (5%)
    all_to_all x3, blocking collectives, gathered(): lax.all_to_all(jnp.broadcast_to(x[None], (count,) + x.shape), axis, 0, 0)  58.9 us
    ppermute x1, waiting for transfers between devices, body(): before = lax.ppermute(feats[nodes - HALF:], GRID, up)  39.9 us
    all_to_all x3, starting transfers between devices, gathered(): lax.all_to_all(jnp.broadcast_to(x[None], (count,) + x.shape), axis, 0, 0)  21.2 us
    ppermute x3, starting transfers between devices, shifted(): lax.ppermute(value, axis, [(i, (i + steps) % count) for i in range(count)])  20.7 us
    all_to_all x3, waiting for transfers between devices, gathered(): lax.all_to_all(jnp.broadcast_to(x[None], (count,) + x.shape), axis, 0, 0)  12.4 us
    all_to_all x1, blocking collectives, total(): piece = jnp.sum(lax.all_to_all(pieces, PLANE, 0, 0).astype(f32), 0)  11.6 us
    pallas_call x1, Pallas kernels, body(): pl.pallas_call(mine_kernel, out_shape=(half, jax.ShapeDtypeStruct((ext, w...  11.5 us
    pallas_call x1, Pallas kernels, body(): pl.pallas_call(other_kernel, out_shape=half, in_specs=[smem, vmem, anywhe...  11.4 us
  transfers between devices with their start and end apart: 8, of which 6 were waited for; matrix products, arithmetic and copies ran while one was open for 1% of the time, Pallas kernels for 11%

profile of v2, /device:TPU:1, one launch (start us, length us, event | category | flops | bytes accessed | tf_op | source)
XLA Modules:
  0.0 217.6 jit_solution(13879159810628532833)
XLA Ops:
  2.4 12.2 %all_to_all.35 = bf16[4,16,2048]{2,1,0:T(8,128)(2,1)S(1)} all-to-all(bf16[4,16,2048]{2,1,0:T(8,128)(2,1)S(1)} %broadcast_in_dim.22), channel_id=1, replica_groups=mesh['z_hi'=4,'core'=2,'y'=4,'z_lo'=4,'x'=4] {'z_lo'}, dimensions={0} | all-to-all | bytes 524288 | tf_op jit(solution)/shard_map/all_to_all | solution.py:248
  14.6 2.1 broadcast_in_dim.23
  16.7 7.8 %all-to-all-start.1 = ((bf16[16,4,16,1536]{3,2,1,0:T(8,128)(2,1)}), bf16[16,4,16,1536]{3,2,1,0:T(8,128)(2,1)}, u32[]{:S(2)}, u32[]{:S(2)}) async-start(bf16[16,4,16,1536]{3,2,1,0:T(8,128)(2,1)} %broadcast_in_dim.23), calls=%async_computation.1 | async-start | bytes 6291456 | tf_op jit(solution)/shard_map/all_to_all | solution.py:248
  24.6 3.3 %collective-permute-start = (bf16[256,1024]{1,0:T(8,128)(2,1)S(1)}, bf16[256,1024]{1,0:T(8,128)(2,1)S(1)}, u32[]{:S(2)}, u32[]{:S(2)}) collective-permute-start(bf16[256,1024]{1,0:T(8,128)(2,1)S(1)} %get-tuple-element.35), channel_id=1, source_target_pairs={{0,1},{1,2},{2,3},{3,4},{4,5},{5,6},{6,7},{7,8},{8,9},{9,10},{10,1... | collective-permute-start | bytes 1572872 | tf_op jit(solution)/shard_map/ppermute | solution.py:267
  27.9 1.3 collective-permute-start.1
  29.2 39.9 %collective-permute-done.before = bf16[256,1024]{1,0:T(8,128)(2,1)S(1)} collective-permute-done((bf16[256,1024]{1,0:T(8,128)(2,1)S(1)}, bf16[256,1024]{1,0:T(8,128)(2,1)S(1)}, u32[]{:S(2)}, u32[]{:S(2)}) %collective-permute-start) | collective-permute-done | bytes 524320 | tf_op jit(solution)/shard_map/ppermute | solution.py:267
  69.1 5.2 %collective-permute-done.1.after = bf16[256,1024]{1,0:T(8,128)(2,1)S(1)} collective-permute-done((bf16[256,1024]{1,0:T(8,128)(2,1)S(1)}, bf16[256,1024]{1,0:T(8,128)(2,1)S(1)}, u32[]{:S(2)}, u32[]{:S(2)}) %collective-permute-start.1) | collective-permute-done | bytes 524320 | tf_op jit(solution)/shard_map/ppermute | solution.py:268
  74.3 1.9 all-to-all-done.1
  76.3 4.0 %collective-permute-start.2 = (bf16[4,4,4,16,1536]{4,3,2,1,0:T(8,128)(2,1)}, bf16[4,4,4,16,1536]{4,3,2,1,0:T(8,128)(2,1)}, u32[]{:S(2)}, u32[]{:S(2)}) collective-permute-start(bf16[4,4,4,16,1536]{4,3,2,1,0:T(8,128)(2,1)} %bitcast.6.gathered_weights), channel_id=1, source_target_pairs={{0,64},{64,0},{1,65},{65,1},{2,66},{66,2},{3,67},{67,3},{4,68},{68... | collective-permute-start | bytes 9437192 | tf_op jit(solution)/shard_map/ppermute | solution.py:243
  81.4 6.0 %all-to-all-start.2 = ((bf16[16,4,16,512]{3,2,1,0:T(8,128)(2,1)}), bf16[16,4,16,512]{3,2,1,0:T(8,128)(2,1)S(1)}, u32[]{:S(2)}, u32[]{:S(2)}) async-start(bf16[16,4,16,512]{3,2,1,0:T(8,128)(2,1)} %broadcast_in_dim.24), calls=%async_computation.2 | async-start | bytes 2097152 | tf_op jit(solution)/shard_map/all_to_all | solution.py:248
  88.7 11.5 %heads_mine.1 = (bf16[512,512]{1,0:T(8,128)(2,1)S(1)}, bf16[1024,1024]{1,0:T(8,128)(2,1)S(1)}) custom-call(s32[3]{0:T(128)S(1)} %pad_add_fusion.edge, bf16[256,1024]{1,0:T(8,128)(2,1)S(1)} %collective-permute-done.before, bf16[512,1024]{1,0:T(8,128)(2,1)S(1)} %bitcast.20, bf16[256,1024]{1,0:T(8,128)(2,1)S(1)} %copy-done.6, ...), custom_call_target="tpu_custom_call" | custom-call | flops 4000000000 | bytes 8000000 | tf_op jit(solution)/shard_map/heads_mine/pallas_call | solution.py:299
  100.2 1.4 copy-done.7
  101.6 3.3 %all-to-all-done.2 = bf16[16,4,16,512]{3,2,1,0:T(8,128)(2,1)S(1)} async-done(((bf16[16,4,16,512]{3,2,1,0:T(8,128)(2,1)}), bf16[16,4,16,512]{3,2,1,0:T(8,128)(2,1)S(1)}, u32[]{:S(2)}, u32[]{:S(2)}) %all-to-all-start.2) | async-done | bytes 1048608 | tf_op jit(solution)/shard_map/all_to_all | solution.py:248
  104.9 3.5 %collective-permute-start.3 = (bf16[4,4,4,16,512]{4,3,2,1,0:T(8,128)(2,1)S(1)}, bf16[4,4,4,16,512]{4,3,2,1,0:T(8,128)(2,1)S(1)}, u32[]{:S(2)}, u32[]{:S(2)}) collective-permute-start(bf16[4,4,4,16,512]{4,3,2,1,0:T(8,128)(2,1)S(1)} %bitcast.22), channel_id=1, source_target_pairs={{0,64},{64,0},{1,65},{65,1},{2,66},{66,2},{3,67},{67,3},{4,68},{68... | collective-permute-start | bytes 3145736 | tf_op jit(solution)/shard_map/ppermute | solution.py:243
  108.5 1.6 copy-done.8
  110.1 11.4 %heads_other.1.attended_other = bf16[512,512]{1,0:T(8,128)(2,1)S(1)} custom-call(s32[3]{0:T(128)S(1)} %pad_add_fusion.edge, bf16[1024,1024]{1,0:T(8,128)(2,1)S(1)} %copy-done.8, bf16[4,4,4,16,1536]{4,3,2,1,0:T(8,128)(2,1)} %collective-permute-done.2.gathered_weights, f32[1,1024]{1,0:T(1,128)S(1)} %broadcast_in_dim_reshape.3.scale), custom_call_target="tpu_custom_call" | custom-call | flops 4000000000 | bytes 8000000 | tf_op jit(solution)/shard_map/heads_other/pallas_call | solution.py:309
  121.5 3.3 %hidden.1 = (bf16[512,1024]{1,0:T(8,128)(2,1)S(1)}, bf16[100,512]{1,0:T(8,128)(2,1)S(1)}) custom-call(s32[3]{0:T(128)S(1)} %pad_add_fusion.edge, bf16[512,1024]{1,0:T(8,128)(2,1)S(1)} %bitcast.21, bf16[512,512]{1,0:T(8,128)(2,1)S(1)} %get-tuple-element.19.attended_mine, bf16[512,512]{1,0:T(8,128)(2,1)S(1)} %heads_other.1.attended_other, ...), custom_call_target="tpu_custom_call" | custom-call | tf_op jit(solution)/shard_map/hidden/pallas_call | solution.py:321
  124.8 30.4 %all_to_all.36.same_core = bf16[4,100,512]{2,1,0:T(8,128)(2,1)S(1)} all-to-all(bf16[4,100,512]{2,1,0:T(8,128)(2,1)S(1)} %broadcast_in_dim.27), channel_id=1, replica_groups=mesh['z_hi'=4,'core'=2,'y'=4,'z_lo'=4,'x'=4] {'z_hi'}, dimensions={0} | all-to-all | bytes 819200 | tf_op jit(solution)/shard_map/all_to_all | solution.py:248
  155.3 13.2 %collective-permute-start.4 = (bf16[4,100,512]{2,1,0:T(8,128)(2,1)S(1)}, bf16[4,100,512]{2,1,0:T(8,128)(2,1)S(1)}, u32[]{:S(2)}, u32[]{:S(2)}) collective-permute-start(bf16[4,100,512]{2,1,0:T(8,128)(2,1)S(1)} %all_to_all.36.same_core), channel_id=1, source_target_pairs={{0,64},{64,0},{1,65},{65,1},{2,66},{66,2},{3,67},{67,3},{4,68},{68... | collective-permute-start | bytes 1228808 | tf_op jit(solution)/shard_map/ppermute | solution.py:243
  169.6 2.7 %score.1 = (f32[100,1024]{1,0:T(8,128)S(1)}, bf16[32,32,128]{2,1,0:T(8,128)(2,1)S(1)}) custom-call(bf16[100,512]{1,0:T(8,128)(2,1)S(1)} %get-tuple-element.22.own, bf16[4,100,512]{2,1,0:T(8,128)(2,1)S(1)} %all_to_all.36.same_core, bf16[4,100,512]{2,1,0:T(8,128)(2,1)S(1)} %collective-permute-done.4.other_core, ...), custom_call_target="tpu_custom_call" | custom-call | tf_op jit(solution)/shard_map/score/pallas_call | solution.py:337
  172.3 11.6 %all_to_all.37 = bf16[32,32,128]{2,1,0:T(8,128)(2,1)S(1)} all-to-all(bf16[32,32,128]{2,1,0:T(8,128)(2,1)S(1)} %get-tuple-element.25), channel_id=1, replica_groups=mesh['z_hi'=4,'core'=2,'y'=4,'z_lo'=4,'x'=4] {'core','y','x'}, dimensions={0} | all-to-all | bytes 524288 | tf_op jit(solution)/shard_map/all_to_all | solution.py:252
  184.0 16.2 %all_to_all.38 = bf16[16,32,128]{2,1,0:T(8,128)(2,1)S(1)} all-to-all(bf16[16,32,128]{2,1,0:T(8,128)(2,1)S(1)} %broadcast_in_dim.60), channel_id=1, replica_groups=mesh['z_hi'=4,'core'=2,'y'=4,'z_lo'=4,'x'=4] {'z_hi','z_lo'}, dimensions={0} | all-to-all | bytes 262144 | tf_op jit(solution)/shard_map/all_to_all | solution.py:248
  200.9 7.4 %all-to-all-start.6 = ((bf16[32,32,128]{2,1,0:T(8,128)(2,1)}), bf16[32,32,128]{2,1,0:T(8,128)(2,1)S(1)}, u32[]{:S(2)}, u32[]{:S(2)}) async-start(bf16[32,32,128]{2,1,0:T(8,128)(2,1)} %broadcast_in_dim.61), calls=%async_computation.6 | async-start | bytes 524288 | tf_op jit(solution)/shard_map/all_to_all | solution.py:248
  209.5 7.1 %all-to-all-done.6 = bf16[32,32,128]{2,1,0:T(8,128)(2,1)S(1)} async-done(((bf16[32,32,128]{2,1,0:T(8,128)(2,1)}), bf16[32,32,128]{2,1,0:T(8,128)(2,1)S(1)}, u32[]{:S(2)}, u32[]{:S(2)}) %all-to-all-start.6) | async-done | bytes 262176 | tf_op jit(solution)/shard_map/all_to_all | solution.py:248
  (50 shorter events, 8.4 us)
Async XLA Ops:
  16.7 7.8 %copy-start = (bf16[1,512,1024]{2,1,0:T(8,128)(2,1)S(1)}, bf16[1,512,1024]{2,1,0:T(8,128)(2,1)}, u32[]{:S(2)}) copy-start(bf16[1,512,1024]{2,1,0:T(8,128)(2,1)} %param.11) | copy-start | bytes 3145732
  16.7 59.6 %all-to-all-start.1 = ((bf16[16,4,16,1536]{3,2,1,0:T(8,128)(2,1)}), bf16[16,4,16,1536]{3,2,1,0:T(8,128)(2,1)}, u32[]{:S(2)}, u32[]{:S(2)}) async-start(bf16[16,4,16,1536]{3,2,1,0:T(8,128)(2,1)} %broadcast_in_dim.23), calls=%async_computation.1 | async-start | bytes 6291456 | tf_op jit(solution)/shard_map/all_to_all | solution.py:248
  24.5 62.9 %copy-start.10 = (f32[16]{0:T(128)S(1)}, f32[16]{0:T(128)}, u32[]{:S(2)}) copy-start(f32[16]{0:T(128)} %param.17) | copy-start | bytes 196
  24.5 63.1 %copy-start.9 = (bf16[1024]{0:T(1024)(128)(2,1)S(1)}, bf16[1024]{0:T(1024)(128)(2,1)}, u32[]{:S(2)}) copy-start(bf16[1024]{0:T(1024)(128)(2,1)} %param.12) | copy-start | bytes 6148
  24.6 44.5 %collective-permute-start = (bf16[256,1024]{1,0:T(8,128)(2,1)S(1)}, bf16[256,1024]{1,0:T(8,128)(2,1)S(1)}, u32[]{:S(2)}, u32[]{:S(2)}) collective-permute-start(bf16[256,1024]{1,0:T(8,128)(2,1)S(1)} %get-tuple-element.35), channel_id=1, source_target_pairs={{0,1},{1,2},{2,3},{3,4},{4,5},{5,6},{6,7},{7,8},{8,9},{9,10},{10,1... | collective-permute-start | bytes 1572872 | tf_op jit(solution)/shard_map/ppermute | solution.py:267
  27.9 46.5 %collective-permute-start.1 = (bf16[256,1024]{1,0:T(8,128)(2,1)S(1)}, bf16[256,1024]{1,0:T(8,128)(2,1)S(1)}, u32[]{:S(2)}, u32[]{:S(2)}) collective-permute-start(bf16[256,1024]{1,0:T(8,128)(2,1)S(1)} %get-tuple-element.34), channel_id=1, source_target_pairs={{1,0},{2,1},{3,2},{4,3},{5,4},{6,5},{7,6},{8,7},{9,8},{10,9},{11,1... | collective-permute-start | bytes 1572872 | tf_op jit(solution)/shard_map/ppermute | solution.py:268
  74.3 7.1 %copy-start.5 = (bf16[256,1024]{1,0:T(8,128)(2,1)}, bf16[256,1024]{1,0:T(8,128)(2,1)S(1)}, u32[]{:S(2)}) copy-start(bf16[256,1024]{1,0:T(8,128)(2,1)S(1)} %collective-permute-done.1.after) | copy-start | bytes 1572868
  76.3 32.2 %collective-permute-start.2 = (bf16[4,4,4,16,1536]{4,3,2,1,0:T(8,128)(2,1)}, bf16[4,4,4,16,1536]{4,3,2,1,0:T(8,128)(2,1)}, u32[]{:S(2)}, u32[]{:S(2)}) collective-permute-start(bf16[4,4,4,16,1536]{4,3,2,1,0:T(8,128)(2,1)} %bitcast.6.gathered_weights), channel_id=1, source_target_pairs={{0,64},{64,0},{1,65},{65,1},{2,66},{66,2},{3,67},{67,3},{4,68},{68... | collective-permute-start | bytes 9437192 | tf_op jit(solution)/shard_map/ppermute | solution.py:243
  81.4 23.5 %all-to-all-start.2 = ((bf16[16,4,16,512]{3,2,1,0:T(8,128)(2,1)}), bf16[16,4,16,512]{3,2,1,0:T(8,128)(2,1)S(1)}, u32[]{:S(2)}, u32[]{:S(2)}) async-start(bf16[16,4,16,512]{3,2,1,0:T(8,128)(2,1)} %broadcast_in_dim.24), calls=%async_computation.2 | async-start | bytes 2097152 | tf_op jit(solution)/shard_map/all_to_all | solution.py:248
  87.7 1.0 copy-start.6
  100.2 1.4 copy-start.7
  104.9 16.6 %collective-permute-start.3 = (bf16[4,4,4,16,512]{4,3,2,1,0:T(8,128)(2,1)S(1)}, bf16[4,4,4,16,512]{4,3,2,1,0:T(8,128)(2,1)S(1)}, u32[]{:S(2)}, u32[]{:S(2)}) collective-permute-start(bf16[4,4,4,16,512]{4,3,2,1,0:T(8,128)(2,1)S(1)} %bitcast.22), channel_id=1, source_target_pairs={{0,64},{64,0},{1,65},{65,1},{2,66},{66,2},{3,67},{67,3},{4,68},{68... | collective-permute-start | bytes 3145736 | tf_op jit(solution)/shard_map/ppermute | solution.py:243
  108.5 1.6 copy-start.8
  110.0 11.4 %copy-start.2 = (bf16[100,1024]{1,0:T(8,128)(2,1)S(1)}, bf16[100,1024]{1,0:T(8,128)(2,1)}, u32[]{:S(2)}) copy-start(bf16[100,1024]{1,0:T(8,128)(2,1)} %w_dec.1) | copy-start | bytes 614404
  121.4 48.2 %copy-start.1 = (bf16[100,1024]{1,0:T(8,128)(2,1)S(1)}, bf16[100,1024]{1,0:T(8,128)(2,1)}, u32[]{:S(2)}) copy-start(bf16[100,1024]{1,0:T(8,128)(2,1)} %targets.1) | copy-start | bytes 614404
  121.5 48.1 %copy-start.3 = (s32[1024]{0:T(1024)S(1)}, s32[1024]{0:T(1024)}, u32[]{:S(2)}) copy-start(s32[1024]{0:T(1024)} %param.20) | copy-start | bytes 12292
  121.5 48.1 %copy-start.4 = (f32[1024]{0:T(1024)S(1)}, f32[1024]{0:T(1024)}, u32[]{:S(2)}) copy-start(f32[1024]{0:T(1024)} %param.21) | copy-start | bytes 12292
  155.3 14.3 %collective-permute-start.4 = (bf16[4,100,512]{2,1,0:T(8,128)(2,1)S(1)}, bf16[4,100,512]{2,1,0:T(8,128)(2,1)S(1)}, u32[]{:S(2)}, u32[]{:S(2)}) collective-permute-start(bf16[4,100,512]{2,1,0:T(8,128)(2,1)S(1)} %all_to_all.36.same_core), channel_id=1, source_target_pairs={{0,64},{64,0},{1,65},{65,1},{2,66},{66,2},{3,67},{67,3},{4,68},{68... | collective-permute-start | bytes 1228808 | tf_op jit(solution)/shard_map/ppermute | solution.py:243
  200.9 15.7 %all-to-all-start.6 = ((bf16[32,32,128]{2,1,0:T(8,128)(2,1)}), bf16[32,32,128]{2,1,0:T(8,128)(2,1)S(1)}, u32[]{:S(2)}, u32[]{:S(2)}) async-start(bf16[32,32,128]{2,1,0:T(8,128)(2,1)} %broadcast_in_dim.61), calls=%async_computation.6 | async-start | bytes 524288 | tf_op jit(solution)/shard_map/all_to_all | solution.py:248

commit v3 on v2

--- a/solution.py
+++ b/solution.py
@@ -15,6 +15,7 @@
 BLOCK = 128
 LOW = -1e30
 MIB = 1024 * 1024
+EARLY = 3
 
 GRID = ("y", "z_lo", "x")
 MEMBER = ("z_hi", "core")
@@ -59,6 +60,20 @@
 
         loop(ref.shape[0] // 64, norm)
         start += ref.shape[0]
+
+
+def lane_tiles(x):
+    whole = x.shape[0] // 16 * 16
+    tiles = [x[:, t * LANES : (t + 1) * LANES] for t in range(x.shape[1] // LANES)]
+    return [tile[:whole] for tile in tiles], jnp.concatenate([tile[whole:] for tile in tiles], 0)
+
+
+def from_lane_tiles(tiles, rest):
+    each = rest.shape[0] // len(tiles)
+    whole = [
+        jnp.concatenate([tile, rest[t * each : (t + 1) * each]], 0) for t, tile in enumerate(tiles)
+    ]
+    return jnp.concatenate(whole, 1)
 
 
 def weight_copies(gathered_weights, weights, sems):
@@ -74,7 +89,8 @@
     return copies
 
 
-def attend_pairs(edge, normed, weights, scale, base, query, keys, values, attended):
+def attend_pairs(edge, normed, weights, scale, half, first, query, keys, values, attended):
+    base = half * (scale.shape[1] // 2) + first * LANES
     ext, width = normed.shape
     nodes = ext - 2 * HALF
     pairs = weights.shape[-1] // (3 * LANES)
@@ -137,60 +153,74 @@
             weight = jnp.concatenate([jnp.exp(part - top).astype(bf16) for part in parts], 1)
             mixed = dot(weight, jnp.concatenate([values[window, cols], ones], 1))
             mixed = mixed[:, :LANES] / mixed[:, LANES:]
-            attended[rows, cols] = jnp.where(first_head, mixed[:BLOCK], mixed[BLOCK:]).astype(bf16)
-
-
-def mine_kernel(
-    edge, before, feats, after, gain, gathered_weights, scale,
-    attended, normed,
-    weights, query, keys, values, sems,
+            out_cols = pl.ds(pl.multiple_of(base + p * LANES, LANES), LANES)
+            attended[rows, out_cols] = jnp.where(first_head, mixed[:BLOCK], mixed[BLOCK:]).astype(bf16)
+
+
+def early_kernel(
+    edge, before, feats, after, gain, gathered_mine, gathered_other, scale,
+    attended, normed_out,
+    normed, weights_mine, weights_other, query, keys, values, sems_mine, sems_other, out_sem,
 ):
-    copies = weight_copies(gathered_weights, weights, sems)
-    for copy in copies:
+    copies_mine = weight_copies(gathered_mine, weights_mine, sems_mine)
+    copies_other = weight_copies(gathered_other, weights_other, sems_other)
+    for copy in copies_mine + copies_other:
         copy.start()
     normalise(before, feats, after, gain, normed)
-    for copy in copies:
-        copy.wait()
-    base = edge[2] * (scale.shape[1] // 2)
-    attend_pairs(edge, normed, weights, scale, base, query, keys, values, attended)
-
-
-def other_kernel(
-    edge, normed, gathered_weights, scale,
-    attended,
-    weights, query, keys, values, sems,
-):
-    copies = weight_copies(gathered_weights, weights, sems)
-    for copy in copies:
-        copy.start()
-    for copy in copies:
-        copy.wait()
-    base = (1 - edge[2]) * (scale.shape[1] // 2)
-    attend_pairs(edge, normed, weights, scale, base, query, keys, values, attended)
-
-
-def hidden_kernel(
-    edge, feats, attended_mine, attended_other, gathered_mine, gathered_other, w_dec,
-    hidden_out, fields_out,
-    out_mine, out_other, sems_mine, sems_other,
+    leave = pltpu.make_async_copy(normed, normed_out, out_sem)
+    leave.start()
+    for i, (half, weights, copies) in enumerate(
+        ((edge[2], weights_mine, copies_mine), (1 - edge[2], weights_other, copies_other))
+    ):
+        for copy in copies:
+            copy.wait()
+        attend_pairs(edge, normed, weights, scale, half, 0, query.at[i], keys.at[i], values.at[i], attended)
+    leave.wait()
+
+
+def late_kernel(
+    edge, feats, normed_in, attended_early, gathered_mine, gathered_other, scale, w_dec,
+    hidden_out, fields_out, packed_out,
+    normed, attended, weights_mine, weights_other, out_mine, out_other, query, keys, values,
+    in_sem, sems_mine, sems_other, sems_out_mine, sems_out_other,
 ):
     nodes, width = feats.shape
     mine = width // 2
-    copies = weight_copies(gathered_mine, out_mine, sems_mine)
-    copies += weight_copies(gathered_other, out_other, sems_other)
-    for copy in copies:
+    columns = weights_mine.shape[-1]
+    heads, out = pl.ds(0, columns), pl.ds(columns, mine)
+    enter = pltpu.make_async_copy(normed_in, normed, in_sem)
+    copies_mine = weight_copies(gathered_mine.at[..., heads], weights_mine, sems_mine)
+    copies_other = weight_copies(gathered_other.at[..., heads], weights_other, sems_other)
+    copies_out = weight_copies(gathered_mine.at[..., out], out_mine, sems_out_mine)
+    copies_out += weight_copies(gathered_other.at[..., out], out_other, sems_out_other)
+    for copy in [enter] + copies_mine + copies_other + copies_out:
         copy.start()
+    attended[...] = attended_early[...]
+    enter.wait()
+    for i, (half, weights, copies) in enumerate(
+        ((edge[2], weights_mine, copies_mine), (1 - edge[2], weights_other, copies_other))
+    ):
+        for copy in copies:
+            copy.wait()
+        attend_pairs(edge, normed, weights, scale, half, EARLY, query.at[i], keys.at[i], values.at[i], attended)
     here = pl.ds(pl.multiple_of(edge[2] * mine, mine), mine)
     there = pl.ds(pl.multiple_of((1 - edge[2]) * mine, mine), mine)
-    for copy in copies:
+    for copy in copies_out:
         copy.wait()
     for half, cols in ((out_mine, here), (out_other, there)):
         flat = half.reshape(width, mine)
         for r in range(nodes // 256):
             rows = pl.ds(r * 256, 256)
-            projected = dot(attended_mine[rows, :], flat[here, :]) + dot(attended_other[rows, :], flat[there, :])
-            hidden_out[rows, cols] = (feats[rows, cols].astype(f32) + projected).astype(bf16)
-    fields_out[...] = dot_t(w_dec[...], hidden_out[...]).astype(bf16)
+            hidden = feats[rows, cols].astype(f32) + dot(attended[rows, :], flat[...])
+            hidden_out[rows, cols] = hidden.astype(bf16)
+    fields = dot_t(w_dec[...], hidden_out[...])
+    fields_out[...] = fields.astype(bf16)
+    tiles, rest = lane_tiles(fields)
+    blocks = tiles[0].shape[0] // 16
+    for t, tile in enumerate(tiles):
+        for i in range(blocks):
+            packed_out[t * blocks + i] = tile[i * 16 : i * 16 + 16].astype(bf16)
+    packed_out[len(tiles) * blocks] = rest.astype(bf16)
 
 
 def score_kernel(
@@ -200,16 +230,27 @@
     members = 2 * same_core.shape[0]
     nodes = own.shape[1]
     variables, cells = targets.shape
-    mine = own[...].astype(f32)
-    spread = jnp.zeros_like(mine) - SMOOTH_SQ**0.5
-    slope = jnp.zeros_like(mine)
-    for ref in (same_core, other_core):
-        for j in range(members // 2):
-            delta = mine - ref[j].astype(f32)
-            square = delta * delta + SMOOTH_SQ
-            inverse = lax.rsqrt(square)
-            spread = spread + square * inverse
-            slope = slope + delta * inverse
+    tiles, rest = lane_tiles(own[...].astype(f32))
+    blocks = tiles[0].shape[0] // 16
+    spreads, slopes = [], []
+    for t, mine in enumerate(tiles + [rest]):
+        spread = jnp.zeros_like(mine) - SMOOTH_SQ**0.5
+        slope = jnp.zeros_like(mine)
+        for ref in (same_core, other_core):
+            for j in range(members // 2):
+                if t < len(tiles):
+                    other = ref[j, t * blocks : (t + 1) * blocks].reshape(mine.shape)
+                else:
+                    other = ref[j, t * blocks]
+                delta = mine - other.astype(f32)
+                square = delta * delta + SMOOTH_SQ
+                inverse = lax.rsqrt(square)
+                spread = spread + square * inverse
+                slope = slope + delta * inverse
+        spreads.append(spread)
+        slopes.append(slope)
+    spread = from_lane_tiles(spreads[:-1], spreads[-1])
+    slope = from_lane_tiles(slopes[:-1], slopes[-1])
     kappa = ALPHA / (2.0 * members * (members - 1)) + (1.0 - ALPHA) / (2.0 * members * members)
     index = lax.broadcasted_iota(jnp.int32, (nodes, cells), 0)
     one_hot = (index == cell_node[...]).astype(bf16)
@@ -243,9 +284,12 @@
     return lax.ppermute(value, axis, [(i, (i + steps) % count) for i in range(count)])
 
 
+def copies_for(x, axis):
+    return jnp.broadcast_to(x[None], (lax.axis_size(axis),) + x.shape)
+
+
 def gathered(x, axis):
-    count = lax.axis_size(axis)
-    return lax.all_to_all(jnp.broadcast_to(x[None], (count,) + x.shape), axis, 0, 0)
+    return lax.all_to_all(copies_for(x, axis), axis, 0, 0)
 
 
 def total(pieces):
@@ -275,14 +319,15 @@
     by_pair = jnp.stack([w.reshape(rows, mine // LANES, LANES) for w in parts[:3]], 2)
     shard = jnp.concatenate([by_pair.reshape(rows, 3 * mine), parts[3]], 1)
     lane = gathered(shard, "z_lo")
-    grouped = lambda w: w.reshape((lax.axis_size("y"), lax.axis_size("x")) + w.shape[1:])
-    heads_mine = gathered(lane[..., : 3 * mine], ("y", "x"))
-    heads_mine, before, after, lane_out = lax.optimization_barrier(
-        (heads_mine, before, after, lane[..., 3 * mine :])
+    plane = gathered(lane, "x")
+    late = mine // LANES - EARLY
+    cut = EARLY * 3 * LANES
+    early_mine = gathered(plane[..., :cut], "y")
+    early_mine, before, after, plane_late = lax.optimization_barrier(
+        (early_mine, before, after, copies_for(plane[..., cut:], "y"))
     )
-    heads_mine = grouped(heads_mine)
-    out_mine = grouped(gathered(lane_out, ("y", "x")))
-    heads_other = shifted(heads_mine, "core", 1)
+    late_mine = lax.all_to_all(plane_late, "y", 0, 0)
+    early_other = shifted(early_mine, "core", 1)
 
     scale = jnp.repeat(head_scale, width // head_scale.shape[0])[None]
     edge = jnp.stack([lax.axis_index(GRID), jnp.int32(shards), core]).astype(jnp.int32)
@@ -292,46 +337,50 @@
     params = pltpu.CompilerParams(vmem_limit_bytes=28 * MIB)
     groups = shards // lax.axis_size("x")
     weights = lambda n: pltpu.VMEM((groups, shards // groups, rows, n), bf16)
-    sems = pltpu.SemaphoreType.DMA((groups,))
-    heads = [pltpu.VMEM((n, mine), bf16) for n in (nodes, ext, ext)]
-    cost = pl.CostEstimate(flops=4_000_000_000, bytes_accessed=8_000_000, transcendentals=0)
-    half = jax.ShapeDtypeStruct((nodes, mine), bf16)
-    attended_mine, normed = pl.pallas_call(
-        mine_kernel,
-        out_shape=(half, jax.ShapeDtypeStruct((ext, width), bf16)),
-        in_specs=[smem] + [vmem] * 4 + [anywhere, vmem],
-        out_specs=(vmem, vmem),
-        scratch_shapes=[weights(3 * mine), *heads, sems],
+    sem, sems = pltpu.SemaphoreType.DMA, pltpu.SemaphoreType.DMA((groups,))
+    extended = pltpu.VMEM((ext, width), bf16)
+    heads = lambda n: [pltpu.VMEM((2, k, n * LANES), bf16) for k in (nodes, ext, ext)]
+    whole = jax.ShapeDtypeStruct((nodes, width), bf16)
+    attended, normed = pl.pallas_call(
+        early_kernel,
+        out_shape=(whole, jax.ShapeDtypeStruct((ext, width), bf16)),
+        in_specs=[smem] + [vmem] * 4 + [anywhere, anywhere, vmem],
+        out_specs=(vmem, anywhere),
+        scratch_shapes=[extended, weights(cut), weights(cut), *heads(EARLY), sems, sems, sem],
         compiler_params=params,
-        cost_estimate=cost,
-        name="heads_mine",
-    )(edge, before, feats, after, norm_gain[None], heads_mine, scale)
-    attended_other = pl.pallas_call(
-        other_kernel,
-        out_shape=half,
-        in_specs=[smem, vmem, anywhere, vmem],
-        out_specs=vmem,
-        scratch_shapes=[weights(3 * mine), *heads, sems],
+        cost_estimate=pl.CostEstimate(flops=8_000_000_000, bytes_accessed=16_000_000, transcendentals=0),
+        name="early_heads",
+    )(edge, before, feats, after, norm_gain[None], early_mine, early_other, scale)
+    late_mine, attended = lax.optimization_barrier((late_mine, attended))
+    late_other = shifted(late_mine, "core", 1)
+    hidden, fields, packed = pl.pallas_call(
+        late_kernel,
+        out_shape=(
+            whole,
+            jax.ShapeDtypeStruct((variables, nodes), bf16),
+            jax.ShapeDtypeStruct((variables * nodes // (16 * LANES), 16, LANES), bf16),
+        ),
+        in_specs=[smem, vmem, anywhere, vmem, anywhere, anywhere, vmem, vmem],
+        out_specs=(vmem, vmem, vmem),
+        scratch_shapes=[
+            extended,
+            pltpu.VMEM((nodes, width), bf16),
+            weights(late * 3 * LANES),
+            weights(late * 3 * LANES),
+            weights(mine),
+            weights(mine),
+            *heads(late),
+            sem,
+            sems,
+            sems,
+            sems,
+            sems,
+        ],
         compiler_params=params,
-        cost_estimate=cost,
-        name="heads_other",
-    )(edge, normed, heads_other, scale)
-    out_mine, attended_mine = lax.optimization_barrier((out_mine, attended_mine))
-    out_other = shifted(out_mine, "core", 1)
-    hidden, fields = pl.pallas_call(
-        hidden_kernel,
-        out_shape=(
-            jax.ShapeDtypeStruct((nodes, width), bf16),
-            jax.ShapeDtypeStruct((variables, nodes), bf16),
-        ),
-        in_specs=[smem, vmem, vmem, vmem, anywhere, anywhere, vmem],
-        out_specs=(vmem, vmem),
-        scratch_shapes=[weights(mine), weights(mine), sems, sems],
-        compiler_params=params,
-        name="hidden",
-    )(edge, feats, attended_mine, attended_other, out_mine, out_other, w_dec)
-
-    same_core = gathered(fields, "z_hi")
+        name="late_heads",
+    )(edge, feats, normed, attended, late_mine, late_other, scale, w_dec)
+
+    same_core = gathered(packed, "z_hi")
     other_core = shifted(same_core, "core", 1)
     pieces = lax.axis_size(PLANE)
     score, grad = pl.pallas_call(

time: 218 us -> 212 us (0.972)
  blocking collectives: 70.4 us -> 87.2 us
  waiting for transfers between devices: 58.7 us -> 43.5 us
  starting transfers between devices: 46.4 us -> 33.8 us
  local copies, waits for them, and re-layouts: 11.2 us -> 16.2 us
    ppermute x1, waiting for transfers between devices: 39.9 us -> 0.01 us  [body(): before = lax.ppermute(feats[nodes - HALF:], GRID, up)]
    all_to_all x3, waiting for transfers between devices: 12.4 us -> 32.3 us  [the longest x2 30.5 us: gathered(): return lax.all_to_all(copies_for(x, axis), axis, 0, 0)]
    all_to_all x3 -> x4, blocking collectives: 58.9 us -> 75.8 us  [gathered(): return lax.all_to_all(copies_for(x, axis), axis, 0, 0)]
    ppermute x3, starting transfers between devices: 20.7 us -> 12.9 us  [shifted(): lax.ppermute(value, axis, [(i, (i + steps) % count) for i in range(count)])]
    all_to_all x3, starting transfers between devices: 21.2 us -> 15.6 us  [the longest x2 12 us: gathered(): return lax.all_to_all(copies_for(x, axis), axis, 0, 0)]
    unnamed x24 -> x32, local copies, waits for them, and re-layouts: 5.24 us -> 10 us
    ppermute x3, waiting for transfers between devices: 1.16 us -> 5.35 us  [shifted(): lax.ppermute(value, axis, [(i, (i + steps) % count) for i in range(count)])]
    pallas_call x3 -> x2, Pallas kernels: 26.1 us -> 25.3 us  [the longest x1 16.6 us: body(): pl.pallas_call(early_kernel, out_shape=(whole, jax.ShapeDtypeStruct((ext,...]
  transfers between devices with their start and end apart: 8 -> 8, of which waited for: 6 -> 7; matrix products, arithmetic and copies ran while one was open for 1% -> 1% of each run, Pallas kernels for 11% -> 8%
where the time goes in v3:
time: 212 us; the launch traced here: 211 us
  blocking collectives  87.2 us (41%)
  waiting for transfers between devices  43.5 us (21%)
  starting transfers between devices  33.8 us (16%)
  Pallas kernels  28 us (13%)
  local copies, waits for them, and re-layouts  16.2 us (8%)
    all_to_all x4, blocking collectives, gathered(): return lax.all_to_all(copies_for(x, axis), axis, 0, 0)  75.8 us
    all_to_all x2, waiting for transfers between devices, gathered(): return lax.all_to_all(copies_for(x, axis), axis, 0, 0)  30.5 us
    pallas_call x1, Pallas kernels, body(): pl.pallas_call(early_kernel, out_shape=(whole, jax.ShapeDtypeStruct((ext,...  16.6 us
    ppermute x3, starting transfers between devices, shifted(): lax.ppermute(value, axis, [(i, (i + steps) % count) for i in range(count)])  12.9 us
    all_to_all x2, starting transfers between devices, gathered(): return lax.all_to_all(copies_for(x, axis), axis, 0, 0)  12 us
    all_to_all x1, blocking collectives, total(): piece = jnp.sum(lax.all_to_all(pieces, PLANE, 0, 0).astype(f32), 0)  11.4 us
    unnamed x32, local copies, waits for them, and re-layouts  10 us
    pallas_call x1, Pallas kernels, body(): pl.pallas_call(late_kernel, out_shape=(whole, jax.ShapeDtypeStruct((varia...  8.76 us
  transfers between devices with their start and end apart: 8, of which 7 were waited for; matrix products, arithmetic and copies ran while one was open for 1% of the time, Pallas kernels for 8%

profile of v3, /device:TPU:1, one launch (start us, length us, event | category | flops | bytes accessed | tf_op | source)
XLA Modules:
  0.0 210.6 jit_solution(2357578060873996594)
XLA Ops:
  2.4 12.2 %all_to_all.40 = bf16[4,16,2048]{2,1,0:T(8,128)(2,1)S(1)} all-to-all(bf16[4,16,2048]{2,1,0:T(8,128)(2,1)S(1)} %broadcast_in_dim.24), channel_id=1, replica_groups=mesh['z_hi'=4,'core'=2,'y'=4,'z_lo'=4,'x'=4] {'z_lo'}, dimensions={0} | all-to-all | bytes 524288 | tf_op jit(solution)/shard_map/all_to_all | solution.py:292
  14.7 16.6 %all_to_all.41 = bf16[4,4,16,2048]{3,2,1,0:T(8,128)(2,1)S(1)} all-to-all(bf16[4,4,16,2048]{3,2,1,0:T(8,128)(2,1)S(1)} %broadcast_in_dim.25), channel_id=1, replica_groups=mesh['z_hi'=4,'core'=2,'y'=4,'z_lo'=4,'x'=4] {'x'}, dimensions={0} | all-to-all | bytes 2097152 | tf_op jit(solution)/shard_map/all_to_all | solution.py:292
  31.4 1.7 broadcast_in_dim.26
  33.1 4.7 %all-to-all-start.2 = ((bf16[4,4,4,16,1152]{4,3,2,1,0:T(8,128)(2,1)}), bf16[4,4,4,16,1152]{4,3,2,1,0:T(8,128)(2,1)}, u32[]{:S(2)}, u32[]{:S(2)}) async-start(bf16[4,4,4,16,1152]{4,3,2,1,0:T(8,128)(2,1)} %broadcast_in_dim.26), calls=%async_computation.2 | async-start | bytes 4718592 | tf_op jit(solution)/shard_map/all_to_all | solution.py:292
  39.1 4.0 %collective-permute-start = (bf16[256,1024]{1,0:T(8,128)(2,1)S(1)}, bf16[256,1024]{1,0:T(8,128)(2,1)S(1)}, u32[]{:S(2)}, u32[]{:S(2)}) collective-permute-start(bf16[256,1024]{1,0:T(8,128)(2,1)S(1)} %get-tuple-element.37), channel_id=1, source_target_pairs={{0,1},{1,2},{2,3},{3,4},{4,5},{5,6},{6,7},{7,8},{8,9},{9,10},{10,1... | collective-permute-start | bytes 1572872 | tf_op jit(solution)/shard_map/ppermute | solution.py:311
  43.2 5.9 %collective-permute-done.1.after = bf16[256,1024]{1,0:T(8,128)(2,1)S(1)} collective-permute-done((bf16[256,1024]{1,0:T(8,128)(2,1)S(1)}, bf16[256,1024]{1,0:T(8,128)(2,1)S(1)}, u32[]{:S(2)}, u32[]{:S(2)}) %collective-permute-start.1) | collective-permute-done | bytes 524320 | tf_op jit(solution)/shard_map/ppermute | solution.py:312
  50.7 23.4 %all-to-all-done.2.gathered_mine = bf16[4,4,4,16,1152]{4,3,2,1,0:T(8,128)(2,1)} async-done(((bf16[4,4,4,16,1152]{4,3,2,1,0:T(8,128)(2,1)}), bf16[4,4,4,16,1152]{4,3,2,1,0:T(8,128)(2,1)}, u32[]{:S(2)}, u32[]{:S(2)}) %all-to-all-start.2) | async-done | bytes 2359328 | tf_op jit(solution)/shard_map/all_to_all | solution.py:292
  74.1 1.5 broadcast_in_dim.27
  75.6 7.1 %collective-permute-start.2 = (bf16[4,4,4,16,1152]{4,3,2,1,0:T(8,128)(2,1)}, bf16[4,4,4,16,1152]{4,3,2,1,0:T(8,128)(2,1)}, u32[]{:S(2)}, u32[]{:S(2)}) collective-permute-start(bf16[4,4,4,16,1152]{4,3,2,1,0:T(8,128)(2,1)} %all-to-all-done.2.gathered_mine), channel_id=1, source_target_pairs={{0,64},{64,0},{1,65},{65,1},{2,66},{66,2},{3,67},{67,3},{4,68},{68... | collective-permute-start | bytes 7077896 | tf_op jit(solution)/shard_map/ppermute | solution.py:284
  82.7 3.6 %all-to-all-start.3 = ((bf16[4,4,4,16,896]{4,3,2,1,0:T(8,128)(2,1)}), bf16[4,4,4,16,896]{4,3,2,1,0:T(8,128)(2,1)S(1)}, u32[]{:S(2)}, u32[]{:S(2)}) async-start(bf16[4,4,4,16,896]{4,3,2,1,0:T(8,128)(2,1)} %broadcast_in_dim.27), calls=%async_computation.3 | async-start | bytes 3670016 | tf_op jit(solution)/shard_map/all_to_all | solution.py:329
  89.3 16.6 %early_heads.1 = (bf16[512,1024]{1,0:T(8,128)(2,1)S(1)}, bf16[1024,1024]{1,0:T(8,128)(2,1)S(1)}) custom-call(s32[3]{0:T(128)S(1)} %pad_add_fusion.edge, bf16[256,1024]{1,0:T(8,128)(2,1)S(1)} %copy-done.12, bf16[512,1024]{1,0:T(8,128)(2,1)S(1)} %bitcast.18, bf16[256,1024]{1,0:T(8,128)(2,1)S(1)} %copy-done.10, bf16[1,1024]{1,0:T(2,128)(2,1)S(1)} %broadcast_in_dim.28.gain, ...), custom_call_target="tpu_custom_call" | custom-call | flops 8000000000 | bytes 16000000 | tf_op jit(solution)/shard_map/early_heads/pallas_call | solution.py:344
  108.1 1.8 all-to-all-done.3.gathered_mine
  109.9 2.7 %collective-permute-start.3 = (bf16[4,4,4,16,896]{4,3,2,1,0:T(8,128)(2,1)S(1)}, bf16[4,4,4,16,896]{4,3,2,1,0:T(8,128)(2,1)S(1)}, u32[]{:S(2)}, u32[]{:S(2)}) collective-permute-start(bf16[4,4,4,16,896]{4,3,2,1,0:T(8,128)(2,1)S(1)} %all-to-all-done.3.gathered_mine), channel_id=1, source_target_pairs={{0,64},{64,0},{1,65},{65,1},{2,66},{66,2},{3,67},{67,3},{4,68},{68... | collective-permute-start | bytes 5505032 | tf_op jit(solution)/shard_map/ppermute | solution.py:284
  112.6 3.4 %collective-permute-done.3.gathered_other = bf16[4,4,4,16,896]{4,3,2,1,0:T(8,128)(2,1)S(1)} collective-permute-done((bf16[4,4,4,16,896]{4,3,2,1,0:T(8,128)(2,1)S(1)}, bf16[4,4,4,16,896]{4,3,2,1,0:T(8,128)(2,1)S(1)}, u32[]{:S(2)}, u32[]{:S(2)}) %collective-permute-start.3) | collective-permute-done | bytes 1835040 | tf_op jit(solution)/shard_map/ppermute | solution.py:284
  116.0 1.6 copy-done.2
  118.9 8.8 %late_heads.1 = (bf16[512,1024]{1,0:T(8,128)(2,1)S(1)}, bf16[100,512]{1,0:T(8,128)(2,1)S(1)}, bf16[25,16,128]{2,1,0:T(8,128)(2,1)S(1)}) custom-call(s32[3]{0:T(128)S(1)} %pad_add_fusion.edge, bf16[512,1024]{1,0:T(8,128)(2,1)S(1)} %bitcast.19, bf16[1024,1024]{1,0:T(8,128)(2,1)S(1)} %copy-done.2, bf16[512,1024]{1,0:T(8,128)(2,1)S(1)} %copy-done.4, ...), custom_call_target="tpu_custom_call" | custom-call | tf_op jit(solution)/shard_map/late_heads/pallas_call | solution.py:356
  127.7 29.3 %all_to_all.42.same_core = bf16[4,25,16,128]{3,2,1,0:T(8,128)(2,1)S(1)} all-to-all(bf16[4,25,16,128]{3,2,1,0:T(8,128)(2,1)S(1)} %broadcast_in_dim.30), channel_id=1, replica_groups=mesh['z_hi'=4,'core'=2,'y'=4,'z_lo'=4,'x'=4] {'z_hi'}, dimensions={0} | all-to-all | bytes 819200 | tf_op jit(solution)/shard_map/all_to_all | solution.py:292
  157.0 3.1 %collective-permute-start.4 = (bf16[4,25,16,128]{3,2,1,0:T(8,128)(2,1)S(1)}, bf16[4,25,16,128]{3,2,1,0:T(8,128)(2,1)S(1)}, u32[]{:S(2)}, u32[]{:S(2)}) collective-permute-start(bf16[4,25,16,128]{3,2,1,0:T(8,128)(2,1)S(1)} %all_to_all.42.same_core), channel_id=1, source_target_pairs={{0,64},{64,0},{1,65},{65,1},{2,66},{66,2},{3,67},{67,3},{4,68},{68... | collective-permute-start | bytes 1228808 | tf_op jit(solution)/shard_map/ppermute | solution.py:284
  160.1 1.4 collective-permute-done.4.other_core
  161.5 2.7 %score.1 = (f32[100,1024]{1,0:T(8,128)S(1)}, bf16[32,32,128]{2,1,0:T(8,128)(2,1)S(1)}) custom-call(bf16[100,512]{1,0:T(8,128)(2,1)S(1)} %get-tuple-element.23.own, bf16[4,25,16,128]{3,2,1,0:T(8,128)(2,1)S(1)} %all_to_all.42.same_core, bf16[4,25,16,128]{3,2,1,0:T(8,128)(2,1)S(1)} %collective-permute-done.4.other_core, ...), custom_call_target="tpu_custom_call" | custom-call | tf_op jit(solution)/shard_map/score/pallas_call | solution.py:386
  164.2 11.4 %all_to_all.43 = bf16[32,32,128]{2,1,0:T(8,128)(2,1)S(1)} all-to-all(bf16[32,32,128]{2,1,0:T(8,128)(2,1)S(1)} %get-tuple-element.27), channel_id=1, replica_groups=mesh['z_hi'=4,'core'=2,'y'=4,'z_lo'=4,'x'=4] {'core','y','x'}, dimensions={0} | all-to-all | bytes 524288 | tf_op jit(solution)/shard_map/all_to_all | solution.py:296
  175.6 17.6 %all_to_all.44 = bf16[16,32,128]{2,1,0:T(8,128)(2,1)S(1)} all-to-all(bf16[16,32,128]{2,1,0:T(8,128)(2,1)S(1)} %broadcast_in_dim.67), channel_id=1, replica_groups=mesh['z_hi'=4,'core'=2,'y'=4,'z_lo'=4,'x'=4] {'z_hi','z_lo'}, dimensions={0} | all-to-all | bytes 262144 | tf_op jit(solution)/shard_map/all_to_all | solution.py:292
  194.0 7.4 %all-to-all-start.7 = ((bf16[32,32,128]{2,1,0:T(8,128)(2,1)}), bf16[32,32,128]{2,1,0:T(8,128)(2,1)S(1)}, u32[]{:S(2)}, u32[]{:S(2)}) async-start(bf16[32,32,128]{2,1,0:T(8,128)(2,1)} %broadcast_in_dim.68), calls=%async_computation.7 | async-start | bytes 524288 | tf_op jit(solution)/shard_map/all_to_all | solution.py:292
  202.5 7.1 %all-to-all-done.7 = bf16[32,32,128]{2,1,0:T(8,128)(2,1)S(1)} async-done(((bf16[32,32,128]{2,1,0:T(8,128)(2,1)}), bf16[32,32,128]{2,1,0:T(8,128)(2,1)S(1)}, u32[]{:S(2)}, u32[]{:S(2)}) %all-to-all-start.7) | async-done | bytes 262176 | tf_op jit(solution)/shard_map/all_to_all | solution.py:292
  (59 shorter events, 14.3 us)
Async XLA Ops:
  33.1 4.7 %copy-start = (bf16[1,512,1024]{2,1,0:T(8,128)(2,1)S(1)}, bf16[1,512,1024]{2,1,0:T(8,128)(2,1)}, u32[]{:S(2)}) copy-start(bf16[1,512,1024]{2,1,0:T(8,128)(2,1)} %param.11) | copy-start | bytes 3145732
  33.1 41.0 %all-to-all-start.2 = ((bf16[4,4,4,16,1152]{4,3,2,1,0:T(8,128)(2,1)}), bf16[4,4,4,16,1152]{4,3,2,1,0:T(8,128)(2,1)}, u32[]{:S(2)}, u32[]{:S(2)}) async-start(bf16[4,4,4,16,1152]{4,3,2,1,0:T(8,128)(2,1)} %broadcast_in_dim.26), calls=%async_computation.2 | async-start | bytes 4718592 | tf_op jit(solution)/shard_map/all_to_all | solution.py:292
  37.8 11.3 %collective-permute-start.1 = (bf16[256,1024]{1,0:T(8,128)(2,1)S(1)}, bf16[256,1024]{1,0:T(8,128)(2,1)S(1)}, u32[]{:S(2)}, u32[]{:S(2)}) collective-permute-start(bf16[256,1024]{1,0:T(8,128)(2,1)S(1)} %get-tuple-element.36), channel_id=1, source_target_pairs={{1,0},{2,1},{3,2},{4,3},{5,4},{6,5},{7,6},{8,7},{9,8},{10,9},{11,1... | collective-permute-start | bytes 1572872 | tf_op jit(solution)/shard_map/ppermute | solution.py:312
  39.1 10.8 %collective-permute-start = (bf16[256,1024]{1,0:T(8,128)(2,1)S(1)}, bf16[256,1024]{1,0:T(8,128)(2,1)S(1)}, u32[]{:S(2)}, u32[]{:S(2)}) collective-permute-start(bf16[256,1024]{1,0:T(8,128)(2,1)S(1)} %get-tuple-element.37), channel_id=1, source_target_pairs={{0,1},{1,2},{2,3},{3,4},{4,5},{5,6},{6,7},{7,8},{8,9},{9,10},{10,1... | collective-permute-start | bytes 1572872 | tf_op jit(solution)/shard_map/ppermute | solution.py:311
  49.1 0.8 copy-start.9
  49.9 0.8 copy-start.11
  75.6 10.7 %copy-start.13 = (bf16[1024]{0:T(1024)(128)(2,1)S(1)}, bf16[1024]{0:T(1024)(128)(2,1)}, u32[]{:S(2)}) copy-start(bf16[1024]{0:T(1024)(128)(2,1)} %param.12) | copy-start | bytes 6148
  75.6 10.7 %copy-start.14 = (f32[16]{0:T(128)S(1)}, f32[16]{0:T(128)}, u32[]{:S(2)}) copy-start(f32[16]{0:T(128)} %param.17) | copy-start | bytes 196
  75.6 11.6 %collective-permute-start.2 = (bf16[4,4,4,16,1152]{4,3,2,1,0:T(8,128)(2,1)}, bf16[4,4,4,16,1152]{4,3,2,1,0:T(8,128)(2,1)}, u32[]{:S(2)}, u32[]{:S(2)}) collective-permute-start(bf16[4,4,4,16,1152]{4,3,2,1,0:T(8,128)(2,1)} %all-to-all-done.2.gathered_mine), channel_id=1, source_target_pairs={{0,64},{64,0},{1,65},{65,1},{2,66},{66,2},{3,67},{67,3},{4,68},{68... | collective-permute-start | bytes 7077896 | tf_op jit(solution)/shard_map/ppermute | solution.py:284
  82.7 27.2 %all-to-all-start.3 = ((bf16[4,4,4,16,896]{4,3,2,1,0:T(8,128)(2,1)}), bf16[4,4,4,16,896]{4,3,2,1,0:T(8,128)(2,1)S(1)}, u32[]{:S(2)}, u32[]{:S(2)}) async-start(bf16[4,4,4,16,896]{4,3,2,1,0:T(8,128)(2,1)} %broadcast_in_dim.27), calls=%async_computation.3 | async-start | bytes 3670016 | tf_op jit(solution)/shard_map/all_to_all | solution.py:329
  87.2 1.0 copy-start.10
  88.2 1.0 copy-start.12
  89.3 26.8 %copy-start.6 = (bf16[100,1024]{1,0:T(8,128)(2,1)S(1)}, bf16[100,1024]{1,0:T(8,128)(2,1)}, u32[]{:S(2)}) copy-start(bf16[100,1024]{1,0:T(8,128)(2,1)} %w_dec.1) | copy-start | bytes 614404
  105.8 1.3 copy-start.1
  107.2 1.0 copy-start.3
  109.9 6.1 %collective-permute-start.3 = (bf16[4,4,4,16,896]{4,3,2,1,0:T(8,128)(2,1)S(1)}, bf16[4,4,4,16,896]{4,3,2,1,0:T(8,128)(2,1)S(1)}, u32[]{:S(2)}, u32[]{:S(2)}) collective-permute-start(bf16[4,4,4,16,896]{4,3,2,1,0:T(8,128)(2,1)S(1)} %all-to-all-done.3.gathered_mine), channel_id=1, source_target_pairs={{0,64},{64,0},{1,65},{65,1},{2,66},{66,2},{3,67},{67,3},{4,68},{68... | collective-permute-start | bytes 5505032 | tf_op jit(solution)/shard_map/ppermute | solution.py:284
  116.0 1.6 copy-start.2
  117.6 1.2 copy-start.4
  118.8 42.6 %copy-start.5 = (bf16[100,1024]{1,0:T(8,128)(2,1)S(1)}, bf16[100,1024]{1,0:T(8,128)(2,1)}, u32[]{:S(2)}) copy-start(bf16[100,1024]{1,0:T(8,128)(2,1)} %targets.1) | copy-start | bytes 614404
  118.9 42.6 %copy-start.7 = (s32[1024]{0:T(1024)S(1)}, s32[1024]{0:T(1024)}, u32[]{:S(2)}) copy-start(s32[1024]{0:T(1024)} %param.20) | copy-start | bytes 12292
  118.9 42.6 %copy-start.8 = (f32[1024]{0:T(1024)S(1)}, f32[1024]{0:T(1024)}, u32[]{:S(2)}) copy-start(f32[1024]{0:T(1024)} %param.21) | copy-start | bytes 12292
  157.0 4.5 %collective-permute-start.4 = (bf16[4,25,16,128]{3,2,1,0:T(8,128)(2,1)S(1)}, bf16[4,25,16,128]{3,2,1,0:T(8,128)(2,1)S(1)}, u32[]{:S(2)}, u32[]{:S(2)}) collective-permute-start(bf16[4,25,16,128]{3,2,1,0:T(8,128)(2,1)S(1)} %all_to_all.42.same_core), channel_id=1, source_target_pairs={{0,64},{64,0},{1,65},{65,1},{2,66},{66,2},{3,67},{67,3},{4,68},{68... | collective-permute-start | bytes 1228808 | tf_op jit(solution)/shard_map/ppermute | solution.py:284
  194.0 15.7 %all-to-all-start.7 = ((bf16[32,32,128]{2,1,0:T(8,128)(2,1)}), bf16[32,32,128]{2,1,0:T(8,128)(2,1)S(1)}, u32[]{:S(2)}, u32[]{:S(2)}) async-start(bf16[32,32,128]{2,1,0:T(8,128)(2,1)} %broadcast_in_dim.68), calls=%async_computation.7 | async-start | bytes 524288 | tf_op jit(solution)/shard_map/all_to_all | solution.py:292

commit v4 on v3

--- a/solution.py
+++ b/solution.py
@@ -16,6 +16,7 @@
 LOW = -1e30
 MIB = 1024 * 1024
 EARLY = 3
+SKEW = 2
 
 GRID = ("y", "z_lo", "x")
 MEMBER = ("z_hi", "core")
@@ -103,7 +104,7 @@
         second = jnp.sum(jnp.where(first_head, 0.0, square), -1, keepdims=True)
         return y * lax.rsqrt(jnp.where(first_head, first, second) + EPS)
 
-    for p in range(pairs):
+    def project(p):
         cols = pl.ds(p * LANES, LANES)
         query_cols = pl.ds(p * 3 * LANES, LANES)
         keyval_cols = pl.ds(p * 3 * LANES + LANES, 2 * LANES)
@@ -125,36 +126,59 @@
     first_head = lax.broadcasted_iota(jnp.int32, (BLOCK, LANES), 1) < 64
     ones = jnp.ones((2 * HALF + BLOCK, LANES), bf16)
     segments = 2 * HALF // BLOCK + 1
+    blocks = nodes // BLOCK
     out_low = jnp.where(edge[0] == 0, LOW, 0.0).astype(f32)
     out_high = jnp.where(edge[0] == edge[1] - 1, LOW, 0.0).astype(f32)
-    for p in range(pairs):
+
+    def scores(p, b):
         cols = pl.ds(p * LANES, LANES)
-        for b in range(nodes // BLOCK):
-            rows = pl.ds(b * BLOCK, BLOCK)
-            window = pl.ds(b * BLOCK, 2 * HALF + BLOCK)
-            q = query[rows, cols]
-            zero = jnp.zeros_like(q)
-            pair = jnp.concatenate([jnp.where(first_head, q, zero), jnp.where(first_head, zero, q)], 0)
-            score = dot_t(pair, keys[window, cols])
-            parts = []
-            for s in range(segments):
-                part = score[:, s * BLOCK : (s + 1) * BLOCK]
-                if s == 0:
-                    part = part + lead
-                if s == segments - 1:
-                    part = part + tail
-                if (b + s + 1) * BLOCK <= HALF:
-                    part = part + out_low
-                if (b + s) * BLOCK >= HALF + nodes:
-                    part = part + out_high
-                parts.append(part)
-            top = functools.reduce(jnp.maximum, parts)
-            top = jnp.max(top, -1, keepdims=True)
-            weight = jnp.concatenate([jnp.exp(part - top).astype(bf16) for part in parts], 1)
-            mixed = dot(weight, jnp.concatenate([values[window, cols], ones], 1))
-            mixed = mixed[:, :LANES] / mixed[:, LANES:]
-            out_cols = pl.ds(pl.multiple_of(base + p * LANES, LANES), LANES)
-            attended[rows, out_cols] = jnp.where(first_head, mixed[:BLOCK], mixed[BLOCK:]).astype(bf16)
+        q = query[pl.ds(b * BLOCK, BLOCK), cols]
+        zero = jnp.zeros_like(q)
+        pair = jnp.concatenate([jnp.where(first_head, q, zero), jnp.where(first_head, zero, q)], 0)
+        score = dot_t(pair, keys[pl.ds(b * BLOCK, 2 * HALF + BLOCK), cols])
+        parts = []
+        for s in range(segments):
+            part = score[:, s * BLOCK : (s + 1) * BLOCK]
+            if s == 0:
+                part = part + lead
+            if s == segments - 1:
+                part = part + tail
+            if (b + s + 1) * BLOCK <= HALF:
+                part = part + out_low
+            if (b + s) * BLOCK >= HALF + nodes:
+                part = part + out_high
+            parts.append(part)
+        return parts
+
+    def softened(parts):
+        top = functools.reduce(jnp.maximum, parts)
+        top = jnp.max(top, -1, keepdims=True)
+        return jnp.concatenate([jnp.exp(part - top).astype(bf16) for part in parts], 1)
+
+    def mix(p, b, weight):
+        window = pl.ds(b * BLOCK, 2 * HALF + BLOCK)
+        value = values[window, pl.ds(p * LANES, LANES)]
+        mixed = dot(weight, jnp.concatenate([value, ones], 1))
+        mixed = mixed[:, :LANES] / mixed[:, LANES:]
+        out_cols = pl.ds(pl.multiple_of(base + p * LANES, LANES), LANES)
+        attended[pl.ds(b * BLOCK, BLOCK), out_cols] = jnp.where(
+            first_head, mixed[:BLOCK], mixed[BLOCK:]
+        ).astype(bf16)
+
+    items = [(p, b) for p in range(pairs) for b in range(blocks)]
+    score, weight = {}, {}
+    project(0)
+    for i in range(len(items) + 2 * SKEW):
+        if i < len(items):
+            if i % blocks == 0 and i // blocks + 1 < pairs:
+                project(i // blocks + 1)
+            score[i] = scores(*items[i])
+        j = i - SKEW
+        if 0 <= j < len(items):
+            weight[j] = softened(score.pop(j))
+        k = j - SKEW
+        if 0 <= k < len(items):
+            mix(*items[k], weight.pop(k))
 
 
 def early_kernel(

time: 212 us -> 211 us (level)
  Pallas kernels: 28 us -> 25 us
  waiting for transfers between devices: 43.5 us -> 45.7 us
    all_to_all x1, waiting for transfers between devices: 1.79 us -> 4.19 us  [body(): late_mine = lax.all_to_all(plane_late, 'y', 0, 0)]
    pallas_call x1, Pallas kernels: 16.6 us -> 14.2 us  [body(): pl.pallas_call(early_kernel, out_shape=(whole, jax.ShapeDtypeStruct((ext,...]
  transfers between devices with their start and end apart: 8 -> 8, of which waited for: 7 -> 7; matrix products, arithmetic and copies ran while one was open for 1% -> 1% of each run, Pallas kernels for 8% -> 7%
where the time goes in v4:
time: 211 us; the launch traced here: 210 us
  blocking collectives  87.1 us (41%)
  waiting for transfers between devices  45.7 us (22%)
  starting transfers between devices  34 us (16%)
  Pallas kernels  25 us (12%)
  local copies, waits for them, and re-layouts  16.2 us (8%)
    all_to_all x4, blocking collectives, gathered(): return lax.all_to_all(copies_for(x, axis), axis, 0, 0)  75.8 us
    all_to_all x2, waiting for transfers between devices, gathered(): return lax.all_to_all(copies_for(x, axis), axis, 0, 0)  30.5 us
    pallas_call x1, Pallas kernels, body(): pl.pallas_call(early_kernel, out_shape=(whole, jax.ShapeDtypeStruct((ext,...  14.2 us
    ppermute x3, starting transfers between devices, shifted(): lax.ppermute(value, axis, [(i, (i + steps) % count) for i in range(count)])  13.1 us
    all_to_all x2, starting transfers between devices, gathered(): return lax.all_to_all(copies_for(x, axis), axis, 0, 0)  12 us
    all_to_all x1, blocking collectives, total(): piece = jnp.sum(lax.all_to_all(pieces, PLANE, 0, 0).astype(f32), 0)  11.4 us
    unnamed x32, local copies, waits for them, and re-layouts  10 us
    pallas_call x1, Pallas kernels, body(): pl.pallas_call(late_kernel, out_shape=(whole, jax.ShapeDtypeStruct((varia...  8.12 us
  transfers between devices with their start and end apart: 8, of which 7 were waited for; matrix products, arithmetic and copies ran while one was open for 1% of the time, Pallas kernels for 7%

profile of v4, /device:TPU:1, one launch (start us, length us, event | category | flops | bytes accessed | tf_op | source)
XLA Modules:
  0.0 209.9 jit_solution(14599424771479397650)
XLA Ops:
  2.4 12.2 %all_to_all.40 = bf16[4,16,2048]{2,1,0:T(8,128)(2,1)S(1)} all-to-all(bf16[4,16,2048]{2,1,0:T(8,128)(2,1)S(1)} %broadcast_in_dim.24), channel_id=1, replica_groups=mesh['z_hi'=4,'core'=2,'y'=4,'z_lo'=4,'x'=4] {'z_lo'}, dimensions={0} | all-to-all | bytes 524288 | tf_op jit(solution)/shard_map/all_to_all | solution.py:316
  14.7 16.6 %all_to_all.41 = bf16[4,4,16,2048]{3,2,1,0:T(8,128)(2,1)S(1)} all-to-all(bf16[4,4,16,2048]{3,2,1,0:T(8,128)(2,1)S(1)} %broadcast_in_dim.25), channel_id=1, replica_groups=mesh['z_hi'=4,'core'=2,'y'=4,'z_lo'=4,'x'=4] {'x'}, dimensions={0} | all-to-all | bytes 2097152 | tf_op jit(solution)/shard_map/all_to_all | solution.py:316
  31.4 1.7 broadcast_in_dim.26
  33.1 4.7 %all-to-all-start.2 = ((bf16[4,4,4,16,1152]{4,3,2,1,0:T(8,128)(2,1)}), bf16[4,4,4,16,1152]{4,3,2,1,0:T(8,128)(2,1)}, u32[]{:S(2)}, u32[]{:S(2)}) async-start(bf16[4,4,4,16,1152]{4,3,2,1,0:T(8,128)(2,1)} %broadcast_in_dim.26), calls=%async_computation.2 | async-start | bytes 4718592 | tf_op jit(solution)/shard_map/all_to_all | solution.py:316
  39.1 4.0 %collective-permute-start = (bf16[256,1024]{1,0:T(8,128)(2,1)S(1)}, bf16[256,1024]{1,0:T(8,128)(2,1)S(1)}, u32[]{:S(2)}, u32[]{:S(2)}) collective-permute-start(bf16[256,1024]{1,0:T(8,128)(2,1)S(1)} %get-tuple-element.37), channel_id=1, source_target_pairs={{0,1},{1,2},{2,3},{3,4},{4,5},{5,6},{6,7},{7,8},{8,9},{9,10},{10,1... | collective-permute-start | bytes 1572872 | tf_op jit(solution)/shard_map/ppermute | solution.py:335
  43.2 5.9 %collective-permute-done.1.after = bf16[256,1024]{1,0:T(8,128)(2,1)S(1)} collective-permute-done((bf16[256,1024]{1,0:T(8,128)(2,1)S(1)}, bf16[256,1024]{1,0:T(8,128)(2,1)S(1)}, u32[]{:S(2)}, u32[]{:S(2)}) %collective-permute-start.1) | collective-permute-done | bytes 524320 | tf_op jit(solution)/shard_map/ppermute | solution.py:336
  50.7 23.4 %all-to-all-done.2.gathered_mine = bf16[4,4,4,16,1152]{4,3,2,1,0:T(8,128)(2,1)} async-done(((bf16[4,4,4,16,1152]{4,3,2,1,0:T(8,128)(2,1)}), bf16[4,4,4,16,1152]{4,3,2,1,0:T(8,128)(2,1)}, u32[]{:S(2)}, u32[]{:S(2)}) %all-to-all-start.2) | async-done | bytes 2359328 | tf_op jit(solution)/shard_map/all_to_all | solution.py:316
  74.1 1.5 broadcast_in_dim.27
  75.6 7.1 %collective-permute-start.2 = (bf16[4,4,4,16,1152]{4,3,2,1,0:T(8,128)(2,1)}, bf16[4,4,4,16,1152]{4,3,2,1,0:T(8,128)(2,1)}, u32[]{:S(2)}, u32[]{:S(2)}) collective-permute-start(bf16[4,4,4,16,1152]{4,3,2,1,0:T(8,128)(2,1)} %all-to-all-done.2.gathered_mine), channel_id=1, source_target_pairs={{0,64},{64,0},{1,65},{65,1},{2,66},{66,2},{3,67},{67,3},{4,68},{68... | collective-permute-start | bytes 7077896 | tf_op jit(solution)/shard_map/ppermute | solution.py:308
  82.7 3.6 %all-to-all-start.3 = ((bf16[4,4,4,16,896]{4,3,2,1,0:T(8,128)(2,1)}), bf16[4,4,4,16,896]{4,3,2,1,0:T(8,128)(2,1)S(1)}, u32[]{:S(2)}, u32[]{:S(2)}) async-start(bf16[4,4,4,16,896]{4,3,2,1,0:T(8,128)(2,1)} %broadcast_in_dim.27), calls=%async_computation.3 | async-start | bytes 3670016 | tf_op jit(solution)/shard_map/all_to_all | solution.py:353
  89.3 14.2 %early_heads.1 = (bf16[512,1024]{1,0:T(8,128)(2,1)S(1)}, bf16[1024,1024]{1,0:T(8,128)(2,1)S(1)}) custom-call(s32[3]{0:T(128)S(1)} %pad_add_fusion.edge, bf16[256,1024]{1,0:T(8,128)(2,1)S(1)} %copy-done.12, bf16[512,1024]{1,0:T(8,128)(2,1)S(1)} %bitcast.18, bf16[256,1024]{1,0:T(8,128)(2,1)S(1)} %copy-done.10, bf16[1,1024]{1,0:T(2,128)(2,1)S(1)} %broadcast_in_dim.28.gain, ...), custom_call_target="tpu_custom_call" | custom-call | flops 8000000000 | bytes 16000000 | tf_op jit(solution)/shard_map/early_heads/pallas_call | solution.py:368
  105.8 4.2 %all-to-all-done.3.gathered_mine = bf16[4,4,4,16,896]{4,3,2,1,0:T(8,128)(2,1)S(1)} async-done(((bf16[4,4,4,16,896]{4,3,2,1,0:T(8,128)(2,1)}), bf16[4,4,4,16,896]{4,3,2,1,0:T(8,128)(2,1)S(1)}, u32[]{:S(2)}, u32[]{:S(2)}) %all-to-all-start.3) | async-done | bytes 1835040 | tf_op jit(solution)/shard_map/all_to_all | solution.py:353
  109.9 2.9 %collective-permute-start.3 = (bf16[4,4,4,16,896]{4,3,2,1,0:T(8,128)(2,1)S(1)}, bf16[4,4,4,16,896]{4,3,2,1,0:T(8,128)(2,1)S(1)}, u32[]{:S(2)}, u32[]{:S(2)}) collective-permute-start(bf16[4,4,4,16,896]{4,3,2,1,0:T(8,128)(2,1)S(1)} %all-to-all-done.3.gathered_mine), channel_id=1, source_target_pairs={{0,64},{64,0},{1,65},{65,1},{2,66},{66,2},{3,67},{67,3},{4,68},{68... | collective-permute-start | bytes 5505032 | tf_op jit(solution)/shard_map/ppermute | solution.py:308
  112.8 3.2 %collective-permute-done.3.gathered_other = bf16[4,4,4,16,896]{4,3,2,1,0:T(8,128)(2,1)S(1)} collective-permute-done((bf16[4,4,4,16,896]{4,3,2,1,0:T(8,128)(2,1)S(1)}, bf16[4,4,4,16,896]{4,3,2,1,0:T(8,128)(2,1)S(1)}, u32[]{:S(2)}, u32[]{:S(2)}) %collective-permute-start.3) | collective-permute-done | bytes 1835040 | tf_op jit(solution)/shard_map/ppermute | solution.py:308
  116.0 1.6 copy-done.2
  118.9 8.1 %late_heads.1 = (bf16[512,1024]{1,0:T(8,128)(2,1)S(1)}, bf16[100,512]{1,0:T(8,128)(2,1)S(1)}, bf16[25,16,128]{2,1,0:T(8,128)(2,1)S(1)}) custom-call(s32[3]{0:T(128)S(1)} %pad_add_fusion.edge, bf16[512,1024]{1,0:T(8,128)(2,1)S(1)} %bitcast.19, bf16[1024,1024]{1,0:T(8,128)(2,1)S(1)} %copy-done.2, bf16[512,1024]{1,0:T(8,128)(2,1)S(1)} %copy-done.4, ...), custom_call_target="tpu_custom_call" | custom-call | tf_op jit(solution)/shard_map/late_heads/pallas_call | solution.py:380
  127.0 29.3 %all_to_all.42.same_core = bf16[4,25,16,128]{3,2,1,0:T(8,128)(2,1)S(1)} all-to-all(bf16[4,25,16,128]{3,2,1,0:T(8,128)(2,1)S(1)} %broadcast_in_dim.30), channel_id=1, replica_groups=mesh['z_hi'=4,'core'=2,'y'=4,'z_lo'=4,'x'=4] {'z_hi'}, dimensions={0} | all-to-all | bytes 819200 | tf_op jit(solution)/shard_map/all_to_all | solution.py:316
  156.3 3.1 %collective-permute-start.4 = (bf16[4,25,16,128]{3,2,1,0:T(8,128)(2,1)S(1)}, bf16[4,25,16,128]{3,2,1,0:T(8,128)(2,1)S(1)}, u32[]{:S(2)}, u32[]{:S(2)}) collective-permute-start(bf16[4,25,16,128]{3,2,1,0:T(8,128)(2,1)S(1)} %all_to_all.42.same_core), channel_id=1, source_target_pairs={{0,64},{64,0},{1,65},{65,1},{2,66},{66,2},{3,67},{67,3},{4,68},{68... | collective-permute-start | bytes 1228808 | tf_op jit(solution)/shard_map/ppermute | solution.py:308
  159.5 1.4 collective-permute-done.4.other_core
  160.8 2.7 %score.1 = (f32[100,1024]{1,0:T(8,128)S(1)}, bf16[32,32,128]{2,1,0:T(8,128)(2,1)S(1)}) custom-call(bf16[100,512]{1,0:T(8,128)(2,1)S(1)} %get-tuple-element.23.own, bf16[4,25,16,128]{3,2,1,0:T(8,128)(2,1)S(1)} %all_to_all.42.same_core, bf16[4,25,16,128]{3,2,1,0:T(8,128)(2,1)S(1)} %collective-permute-done.4.other_core, ...), custom_call_target="tpu_custom_call" | custom-call | tf_op jit(solution)/shard_map/score/pallas_call | solution.py:410
  163.5 11.4 %all_to_all.43 = bf16[32,32,128]{2,1,0:T(8,128)(2,1)S(1)} all-to-all(bf16[32,32,128]{2,1,0:T(8,128)(2,1)S(1)} %get-tuple-element.27), channel_id=1, replica_groups=mesh['z_hi'=4,'core'=2,'y'=4,'z_lo'=4,'x'=4] {'core','y','x'}, dimensions={0} | all-to-all | bytes 524288 | tf_op jit(solution)/shard_map/all_to_all | solution.py:320
  175.0 17.6 %all_to_all.44 = bf16[16,32,128]{2,1,0:T(8,128)(2,1)S(1)} all-to-all(bf16[16,32,128]{2,1,0:T(8,128)(2,1)S(1)} %broadcast_in_dim.67), channel_id=1, replica_groups=mesh['z_hi'=4,'core'=2,'y'=4,'z_lo'=4,'x'=4] {'z_hi','z_lo'}, dimensions={0} | all-to-all | bytes 262144 | tf_op jit(solution)/shard_map/all_to_all | solution.py:316
  193.4 7.4 %all-to-all-start.7 = ((bf16[32,32,128]{2,1,0:T(8,128)(2,1)}), bf16[32,32,128]{2,1,0:T(8,128)(2,1)S(1)}, u32[]{:S(2)}, u32[]{:S(2)}) async-start(bf16[32,32,128]{2,1,0:T(8,128)(2,1)} %broadcast_in_dim.68), calls=%async_computation.7 | async-start | bytes 524288 | tf_op jit(solution)/shard_map/all_to_all | solution.py:316
  201.9 7.1 %all-to-all-done.7 = bf16[32,32,128]{2,1,0:T(8,128)(2,1)S(1)} async-done(((bf16[32,32,128]{2,1,0:T(8,128)(2,1)}), bf16[32,32,128]{2,1,0:T(8,128)(2,1)S(1)}, u32[]{:S(2)}, u32[]{:S(2)}) %all-to-all-start.7) | async-done | bytes 262176 | tf_op jit(solution)/shard_map/all_to_all | solution.py:316
  (59 shorter events, 14.3 us)
Async XLA Ops:
  33.1 4.7 %copy-start = (bf16[1,512,1024]{2,1,0:T(8,128)(2,1)S(1)}, bf16[1,512,1024]{2,1,0:T(8,128)(2,1)}, u32[]{:S(2)}) copy-start(bf16[1,512,1024]{2,1,0:T(8,128)(2,1)} %param.11) | copy-start | bytes 3145732
  33.1 41.0 %all-to-all-start.2 = ((bf16[4,4,4,16,1152]{4,3,2,1,0:T(8,128)(2,1)}), bf16[4,4,4,16,1152]{4,3,2,1,0:T(8,128)(2,1)}, u32[]{:S(2)}, u32[]{:S(2)}) async-start(bf16[4,4,4,16,1152]{4,3,2,1,0:T(8,128)(2,1)} %broadcast_in_dim.26), calls=%async_computation.2 | async-start | bytes 4718592 | tf_op jit(solution)/shard_map/all_to_all | solution.py:316
  37.8 11.3 %collective-permute-start.1 = (bf16[256,1024]{1,0:T(8,128)(2,1)S(1)}, bf16[256,1024]{1,0:T(8,128)(2,1)S(1)}, u32[]{:S(2)}, u32[]{:S(2)}) collective-permute-start(bf16[256,1024]{1,0:T(8,128)(2,1)S(1)} %get-tuple-element.36), channel_id=1, source_target_pairs={{1,0},{2,1},{3,2},{4,3},{5,4},{6,5},{7,6},{8,7},{9,8},{10,9},{11,1... | collective-permute-start | bytes 1572872 | tf_op jit(solution)/shard_map/ppermute | solution.py:336
  39.1 10.8 %collective-permute-start = (bf16[256,1024]{1,0:T(8,128)(2,1)S(1)}, bf16[256,1024]{1,0:T(8,128)(2,1)S(1)}, u32[]{:S(2)}, u32[]{:S(2)}) collective-permute-start(bf16[256,1024]{1,0:T(8,128)(2,1)S(1)} %get-tuple-element.37), channel_id=1, source_target_pairs={{0,1},{1,2},{2,3},{3,4},{4,5},{5,6},{6,7},{7,8},{8,9},{9,10},{10,1... | collective-permute-start | bytes 1572872 | tf_op jit(solution)/shard_map/ppermute | solution.py:335
  49.1 0.8 copy-start.9
  49.9 0.8 copy-start.11
  75.6 10.7 %copy-start.13 = (bf16[1024]{0:T(1024)(128)(2,1)S(1)}, bf16[1024]{0:T(1024)(128)(2,1)}, u32[]{:S(2)}) copy-start(bf16[1024]{0:T(1024)(128)(2,1)} %param.12) | copy-start | bytes 6148
  75.6 10.7 %copy-start.14 = (f32[16]{0:T(128)S(1)}, f32[16]{0:T(128)}, u32[]{:S(2)}) copy-start(f32[16]{0:T(128)} %param.17) | copy-start | bytes 196
  75.6 11.6 %collective-permute-start.2 = (bf16[4,4,4,16,1152]{4,3,2,1,0:T(8,128)(2,1)}, bf16[4,4,4,16,1152]{4,3,2,1,0:T(8,128)(2,1)}, u32[]{:S(2)}, u32[]{:S(2)}) collective-permute-start(bf16[4,4,4,16,1152]{4,3,2,1,0:T(8,128)(2,1)} %all-to-all-done.2.gathered_mine), channel_id=1, source_target_pairs={{0,64},{64,0},{1,65},{65,1},{2,66},{66,2},{3,67},{67,3},{4,68},{68... | collective-permute-start | bytes 7077896 | tf_op jit(solution)/shard_map/ppermute | solution.py:308
  82.7 27.2 %all-to-all-start.3 = ((bf16[4,4,4,16,896]{4,3,2,1,0:T(8,128)(2,1)}), bf16[4,4,4,16,896]{4,3,2,1,0:T(8,128)(2,1)S(1)}, u32[]{:S(2)}, u32[]{:S(2)}) async-start(bf16[4,4,4,16,896]{4,3,2,1,0:T(8,128)(2,1)} %broadcast_in_dim.27), calls=%async_computation.3 | async-start | bytes 3670016 | tf_op jit(solution)/shard_map/all_to_all | solution.py:353
  87.2 1.0 copy-start.10
  88.2 1.0 copy-start.12
  89.3 26.8 %copy-start.6 = (bf16[100,1024]{1,0:T(8,128)(2,1)S(1)}, bf16[100,1024]{1,0:T(8,128)(2,1)}, u32[]{:S(2)}) copy-start(bf16[100,1024]{1,0:T(8,128)(2,1)} %w_dec.1) | copy-start | bytes 614404
  103.4 1.3 copy-start.1
  104.8 1.0 copy-start.3
  109.9 6.1 %collective-permute-start.3 = (bf16[4,4,4,16,896]{4,3,2,1,0:T(8,128)(2,1)S(1)}, bf16[4,4,4,16,896]{4,3,2,1,0:T(8,128)(2,1)S(1)}, u32[]{:S(2)}, u32[]{:S(2)}) collective-permute-start(bf16[4,4,4,16,896]{4,3,2,1,0:T(8,128)(2,1)S(1)} %all-to-all-done.3.gathered_mine), channel_id=1, source_target_pairs={{0,64},{64,0},{1,65},{65,1},{2,66},{66,2},{3,67},{67,3},{4,68},{68... | collective-permute-start | bytes 5505032 | tf_op jit(solution)/shard_map/ppermute | solution.py:308
  116.0 1.6 copy-start.2
  117.6 1.2 copy-start.4
  118.8 42.0 %copy-start.5 = (bf16[100,1024]{1,0:T(8,128)(2,1)S(1)}, bf16[100,1024]{1,0:T(8,128)(2,1)}, u32[]{:S(2)}) copy-start(bf16[100,1024]{1,0:T(8,128)(2,1)} %targets.1) | copy-start | bytes 614404
  118.9 42.0 %copy-start.7 = (s32[1024]{0:T(1024)S(1)}, s32[1024]{0:T(1024)}, u32[]{:S(2)}) copy-start(s32[1024]{0:T(1024)} %param.20) | copy-start | bytes 12292
  118.9 42.0 %copy-start.8 = (f32[1024]{0:T(1024)S(1)}, f32[1024]{0:T(1024)}, u32[]{:S(2)}) copy-start(f32[1024]{0:T(1024)} %param.21) | copy-start | bytes 12292
  156.3 4.5 %collective-permute-start.4 = (bf16[4,25,16,128]{3,2,1,0:T(8,128)(2,1)S(1)}, bf16[4,25,16,128]{3,2,1,0:T(8,128)(2,1)S(1)}, u32[]{:S(2)}, u32[]{:S(2)}) collective-permute-start(bf16[4,25,16,128]{3,2,1,0:T(8,128)(2,1)S(1)} %all_to_all.42.same_core), channel_id=1, source_target_pairs={{0,64},{64,0},{1,65},{65,1},{2,66},{66,2},{3,67},{67,3},{4,68},{68... | collective-permute-start | bytes 1228808 | tf_op jit(solution)/shard_map/ppermute | solution.py:308
  193.4 15.7 %all-to-all-start.7 = ((bf16[32,32,128]{2,1,0:T(8,128)(2,1)}), bf16[32,32,128]{2,1,0:T(8,128)(2,1)S(1)}, u32[]{:S(2)}, u32[]{:S(2)}) async-start(bf16[32,32,128]{2,1,0:T(8,128)(2,1)} %broadcast_in_dim.68), calls=%async_computation.7 | async-start | bytes 524288 | tf_op jit(solution)/shard_map/all_to_all | solution.py:316

commit v5 on v4

--- a/solution.py
+++ b/solution.py
@@ -247,13 +247,31 @@
     packed_out[len(tiles) * blocks] = rest.astype(bf16)
 
 
+def one_hot_cells(cell_node, nodes):
+    index = lax.broadcasted_iota(jnp.int32, (nodes, cell_node.shape[1]), 0)
+    return (index == cell_node[...]).astype(bf16)
+
+
+def error_kernel(members, own, targets, cell_node, cell_area, error_out, node_out, area_out):
+    one_hot = one_hot_cells(cell_node, own.shape[1])
+    fields = dot(own[...], one_hot)
+    error = fields - targets[...].astype(f32)
+    square = error * error + SMOOTH_SQ
+    inverse = lax.rsqrt(square)
+    error_out[...] = square * inverse * (1.0 / members)
+    area = cell_area[...]
+    high, low = halves(area * (error * inverse) * (1.0 / members))
+    area_high, area_low = halves(jnp.broadcast_to(area, area_out.shape[:1] + area.shape[1:]))
+    node_out[...] = dot_t(high, one_hot) + dot_t(low, one_hot)
+    area_out[...] = dot_t(area_high, one_hot) + dot_t(area_low, one_hot)
+
+
 def score_kernel(
-    own, same_core, other_core, hidden, targets, cell_node, cell_area,
+    own, same_core, other_core, hidden, cell_node, error_part, node_part, node_area,
     score_out, grad_out,
 ):
     members = 2 * same_core.shape[0]
-    nodes = own.shape[1]
-    variables, cells = targets.shape
+    variables, nodes = own.shape
     tiles, rest = lane_tiles(own[...].astype(f32))
     blocks = tiles[0].shape[0] // 16
     spreads, slopes = [], []
@@ -276,21 +294,11 @@
     spread = from_lane_tiles(spreads[:-1], spreads[-1])
     slope = from_lane_tiles(slopes[:-1], slopes[-1])
     kappa = ALPHA / (2.0 * members * (members - 1)) + (1.0 - ALPHA) / (2.0 * members * members)
-    index = lax.broadcasted_iota(jnp.int32, (nodes, cells), 0)
-    one_hot = (index == cell_node[...]).astype(bf16)
+    one_hot = one_hot_cells(cell_node, nodes)
     high, low = halves(spread)
-    fields = dot(own[...], one_hot)
     spread = dot(high, one_hot) + dot(low, one_hot)
-    error = fields - targets[...].astype(f32)
-    square = error * error + SMOOTH_SQ
-    inverse = lax.rsqrt(square)
-    score_out[...] = square * inverse * (1.0 / members) - kappa * spread
-    area = cell_area[...]
-    high, low = halves(area * (error * inverse) * (1.0 / members))
-    area_high, area_low = halves(jnp.broadcast_to(area, (8, cells)))
-    node_grad = dot_t(high, one_hot) + dot_t(low, one_hot)
-    node_area = dot_t(area_high, one_hot) + dot_t(area_low, one_hot)
-    node_grad = node_grad - (2.0 * kappa) * slope * node_area[:1]
+    score_out[...] = error_part[...] - kappa * spread
+    node_grad = node_part[...] - (2.0 * kappa) * slope * node_area[:1, :]
     grad = dot(node_grad.astype(bf16), hidden[...])
     tiles = grad.shape[1] // LANES
     each = grad_out.shape[1] // 16
@@ -404,6 +412,19 @@
         name="late_heads",
     )(edge, feats, normed, attended, late_mine, late_other, scale, w_dec)
 
+    members = lax.axis_size(MEMBER)
+    error_part, node_part, node_area = pl.pallas_call(
+        functools.partial(error_kernel, members),
+        out_shape=(
+            jax.ShapeDtypeStruct(targets.shape, f32),
+            jax.ShapeDtypeStruct((variables, nodes), f32),
+            jax.ShapeDtypeStruct((8, nodes), f32),
+        ),
+        in_specs=[vmem] * 4,
+        out_specs=(vmem, vmem, vmem),
+        compiler_params=params,
+        name="error",
+    )(fields, targets, cell_node[None], cell_area[None])
     same_core = gathered(packed, "z_hi")
     other_core = shifted(same_core, "core", 1)
     pieces = lax.axis_size(PLANE)
@@ -413,11 +434,11 @@
             jax.ShapeDtypeStruct(targets.shape, f32),
             jax.ShapeDtypeStruct((pieces, width // pieces, LANES), bf16),
         ),
-        in_specs=[vmem] * 7,
+        in_specs=[vmem] * 8,
         out_specs=(vmem, vmem),
         compiler_params=params,
         name="score",
-    )(fields, same_core, other_core, hidden, targets, cell_node[None], cell_area[None])
+    )(fields, same_core, other_core, hidden, cell_node[None], error_part, node_part, node_area)
     grad = total(grad).reshape(8, width // LANES, 16, LANES).transpose(0, 2, 1, 3)
     return score[None], grad.reshape(128, width)[:variables]
 

time: 211 us -> 210 us (level)
  transfers between devices with their start and end apart: 8 -> 8, of which waited for: 7 -> 6; matrix products, arithmetic and copies ran while one was open for 1% -> 1% of each run, Pallas kernels for 7% -> 8%
where the time goes in v5:
time: 210 us; the launch traced here: 209 us
  blocking collectives  86.9 us (41%)
  waiting for transfers between devices  44.4 us (21%)
  starting transfers between devices  34 us (16%)
  Pallas kernels  25.2 us (12%)
  local copies, waits for them, and re-layouts  16.2 us (8%)
    all_to_all x4, blocking collectives, gathered(): return lax.all_to_all(copies_for(x, axis), axis, 0, 0)  75.8 us
    all_to_all x2, waiting for transfers between devices, gathered(): return lax.all_to_all(copies_for(x, axis), axis, 0, 0)  30.5 us
    pallas_call x1, Pallas kernels, body(): pl.pallas_call(early_kernel, out_shape=(whole, jax.ShapeDtypeStruct((ext,...  14.2 us
    ppermute x3, starting transfers between devices, shifted(): lax.ppermute(value, axis, [(i, (i + steps) % count) for i in range(count)])  13.1 us
    all_to_all x2, starting transfers between devices, gathered(): return lax.all_to_all(copies_for(x, axis), axis, 0, 0)  12 us
    all_to_all x1, blocking collectives, total(): piece = jnp.sum(lax.all_to_all(pieces, PLANE, 0, 0).astype(f32), 0)  11.1 us
    unnamed x32, local copies, waits for them, and re-layouts  10 us
    pallas_call x1, Pallas kernels, body(): pl.pallas_call(late_kernel, out_shape=(whole, jax.ShapeDtypeStruct((varia...  8.11 us
  transfers between devices with their start and end apart: 8, of which 6 were waited for; matrix products, arithmetic and copies ran while one was open for 1% of the time, Pallas kernels for 8%

profile of v5, /device:TPU:1, one launch (start us, length us, event | category | flops | bytes accessed | tf_op | source)
XLA Modules:
  0.0 208.6 jit_solution(17219578773278990053)
XLA Ops:
  2.4 12.2 %all_to_all.40 = bf16[4,16,2048]{2,1,0:T(8,128)(2,1)S(1)} all-to-all(bf16[4,16,2048]{2,1,0:T(8,128)(2,1)S(1)} %broadcast_in_dim.24), channel_id=1, replica_groups=mesh['z_hi'=4,'core'=2,'y'=4,'z_lo'=4,'x'=4] {'z_lo'}, dimensions={0} | all-to-all | bytes 524288 | tf_op jit(solution)/shard_map/all_to_all | solution.py:324
  14.7 16.6 %all_to_all.41 = bf16[4,4,16,2048]{3,2,1,0:T(8,128)(2,1)S(1)} all-to-all(bf16[4,4,16,2048]{3,2,1,0:T(8,128)(2,1)S(1)} %broadcast_in_dim.25), channel_id=1, replica_groups=mesh['z_hi'=4,'core'=2,'y'=4,'z_lo'=4,'x'=4] {'x'}, dimensions={0} | all-to-all | bytes 2097152 | tf_op jit(solution)/shard_map/all_to_all | solution.py:324
  31.4 1.7 broadcast_in_dim.26
  33.1 4.7 %all-to-all-start.2 = ((bf16[4,4,4,16,1152]{4,3,2,1,0:T(8,128)(2,1)}), bf16[4,4,4,16,1152]{4,3,2,1,0:T(8,128)(2,1)}, u32[]{:S(2)}, u32[]{:S(2)}) async-start(bf16[4,4,4,16,1152]{4,3,2,1,0:T(8,128)(2,1)} %broadcast_in_dim.26), calls=%async_computation.2 | async-start | bytes 4718592 | tf_op jit(solution)/shard_map/all_to_all | solution.py:324
  39.1 4.0 %collective-permute-start = (bf16[256,1024]{1,0:T(8,128)(2,1)S(1)}, bf16[256,1024]{1,0:T(8,128)(2,1)S(1)}, u32[]{:S(2)}, u32[]{:S(2)}) collective-permute-start(bf16[256,1024]{1,0:T(8,128)(2,1)S(1)} %get-tuple-element.43), channel_id=1, source_target_pairs={{0,1},{1,2},{2,3},{3,4},{4,5},{5,6},{6,7},{7,8},{8,9},{9,10},{10,1... | collective-permute-start | bytes 1572872 | tf_op jit(solution)/shard_map/ppermute | solution.py:343
  43.2 5.9 %collective-permute-done.1.after = bf16[256,1024]{1,0:T(8,128)(2,1)S(1)} collective-permute-done((bf16[256,1024]{1,0:T(8,128)(2,1)S(1)}, bf16[256,1024]{1,0:T(8,128)(2,1)S(1)}, u32[]{:S(2)}, u32[]{:S(2)}) %collective-permute-start.1) | collective-permute-done | bytes 524320 | tf_op jit(solution)/shard_map/ppermute | solution.py:344
  50.7 23.4 %all-to-all-done.2.gathered_mine = bf16[4,4,4,16,1152]{4,3,2,1,0:T(8,128)(2,1)} async-done(((bf16[4,4,4,16,1152]{4,3,2,1,0:T(8,128)(2,1)}), bf16[4,4,4,16,1152]{4,3,2,1,0:T(8,128)(2,1)}, u32[]{:S(2)}, u32[]{:S(2)}) %all-to-all-start.2) | async-done | bytes 2359328 | tf_op jit(solution)/shard_map/all_to_all | solution.py:324
  74.1 1.5 broadcast_in_dim.27
  75.6 7.1 %collective-permute-start.2 = (bf16[4,4,4,16,1152]{4,3,2,1,0:T(8,128)(2,1)}, bf16[4,4,4,16,1152]{4,3,2,1,0:T(8,128)(2,1)}, u32[]{:S(2)}, u32[]{:S(2)}) collective-permute-start(bf16[4,4,4,16,1152]{4,3,2,1,0:T(8,128)(2,1)} %all-to-all-done.2.gathered_mine), channel_id=1, source_target_pairs={{0,64},{64,0},{1,65},{65,1},{2,66},{66,2},{3,67},{67,3},{4,68},{68... | collective-permute-start | bytes 7077896 | tf_op jit(solution)/shard_map/ppermute | solution.py:316
  82.7 3.6 %all-to-all-start.3 = ((bf16[4,4,4,16,896]{4,3,2,1,0:T(8,128)(2,1)}), bf16[4,4,4,16,896]{4,3,2,1,0:T(8,128)(2,1)S(1)}, u32[]{:S(2)}, u32[]{:S(2)}) async-start(bf16[4,4,4,16,896]{4,3,2,1,0:T(8,128)(2,1)} %broadcast_in_dim.27), calls=%async_computation.3 | async-start | bytes 3670016 | tf_op jit(solution)/shard_map/all_to_all | solution.py:361
  89.3 14.2 %early_heads.1 = (bf16[512,1024]{1,0:T(8,128)(2,1)S(1)}, bf16[1024,1024]{1,0:T(8,128)(2,1)S(1)}) custom-call(s32[3]{0:T(128)S(1)} %pad_add_fusion.edge, bf16[256,1024]{1,0:T(8,128)(2,1)S(1)} %copy-done.12, bf16[512,1024]{1,0:T(8,128)(2,1)S(1)} %bitcast.18, bf16[256,1024]{1,0:T(8,128)(2,1)S(1)} %copy-done.10, bf16[1,1024]{1,0:T(2,128)(2,1)S(1)} %broadcast_in_dim.28.gain, ...), custom_call_target="tpu_custom_call" | custom-call | flops 8000000000 | bytes 16000000 | tf_op jit(solution)/shard_map/early_heads/pallas_call | solution.py:376
  105.8 4.2 %all-to-all-done.3.gathered_mine = bf16[4,4,4,16,896]{4,3,2,1,0:T(8,128)(2,1)S(1)} async-done(((bf16[4,4,4,16,896]{4,3,2,1,0:T(8,128)(2,1)}), bf16[4,4,4,16,896]{4,3,2,1,0:T(8,128)(2,1)S(1)}, u32[]{:S(2)}, u32[]{:S(2)}) %all-to-all-start.3) | async-done | bytes 1835040 | tf_op jit(solution)/shard_map/all_to_all | solution.py:361
  109.9 2.9 %collective-permute-start.3 = (bf16[4,4,4,16,896]{4,3,2,1,0:T(8,128)(2,1)S(1)}, bf16[4,4,4,16,896]{4,3,2,1,0:T(8,128)(2,1)S(1)}, u32[]{:S(2)}, u32[]{:S(2)}) collective-permute-start(bf16[4,4,4,16,896]{4,3,2,1,0:T(8,128)(2,1)S(1)} %all-to-all-done.3.gathered_mine), channel_id=1, source_target_pairs={{0,64},{64,0},{1,65},{65,1},{2,66},{66,2},{3,67},{67,3},{4,68},{68... | collective-permute-start | bytes 5505032 | tf_op jit(solution)/shard_map/ppermute | solution.py:316
  112.8 3.2 %collective-permute-done.3.gathered_other = bf16[4,4,4,16,896]{4,3,2,1,0:T(8,128)(2,1)S(1)} collective-permute-done((bf16[4,4,4,16,896]{4,3,2,1,0:T(8,128)(2,1)S(1)}, bf16[4,4,4,16,896]{4,3,2,1,0:T(8,128)(2,1)S(1)}, u32[]{:S(2)}, u32[]{:S(2)}) %collective-permute-start.3) | collective-permute-done | bytes 1835040 | tf_op jit(solution)/shard_map/ppermute | solution.py:316
  116.0 1.6 copy-done.2
  118.9 8.1 %late_heads.1 = (bf16[512,1024]{1,0:T(8,128)(2,1)S(1)}, bf16[100,512]{1,0:T(8,128)(2,1)S(1)}, bf16[25,16,128]{2,1,0:T(8,128)(2,1)S(1)}) custom-call(s32[3]{0:T(128)S(1)} %pad_add_fusion.edge, bf16[512,1024]{1,0:T(8,128)(2,1)S(1)} %bitcast.19, bf16[1024,1024]{1,0:T(8,128)(2,1)S(1)} %copy-done.2, bf16[512,1024]{1,0:T(8,128)(2,1)S(1)} %copy-done.4, ...), custom_call_target="tpu_custom_call" | custom-call | tf_op jit(solution)/shard_map/late_heads/pallas_call | solution.py:388
  127.0 29.3 %all_to_all.42.same_core = bf16[4,25,16,128]{3,2,1,0:T(8,128)(2,1)S(1)} all-to-all(bf16[4,25,16,128]{3,2,1,0:T(8,128)(2,1)S(1)} %broadcast_in_dim.30), channel_id=1, replica_groups=mesh['z_hi'=4,'core'=2,'y'=4,'z_lo'=4,'x'=4] {'z_hi'}, dimensions={0} | all-to-all | bytes 819200 | tf_op jit(solution)/shard_map/all_to_all | solution.py:324
  156.4 3.1 %collective-permute-start.4 = (bf16[4,25,16,128]{3,2,1,0:T(8,128)(2,1)S(1)}, bf16[4,25,16,128]{3,2,1,0:T(8,128)(2,1)S(1)}, u32[]{:S(2)}, u32[]{:S(2)}) collective-permute-start(bf16[4,25,16,128]{3,2,1,0:T(8,128)(2,1)S(1)} %all_to_all.42.same_core), channel_id=1, source_target_pairs={{0,64},{64,0},{1,65},{65,1},{2,66},{66,2},{3,67},{67,3},{4,68},{68... | collective-permute-start | bytes 1228808 | tf_op jit(solution)/shard_map/ppermute | solution.py:316
  159.5 1.6 error.1
  161.1 1.4 score.1
  162.4 11.1 %all_to_all.43 = bf16[32,32,128]{2,1,0:T(8,128)(2,1)S(1)} all-to-all(bf16[32,32,128]{2,1,0:T(8,128)(2,1)S(1)} %get-tuple-element.33), channel_id=1, replica_groups=mesh['z_hi'=4,'core'=2,'y'=4,'z_lo'=4,'x'=4] {'core','y','x'}, dimensions={0} | all-to-all | bytes 524288 | tf_op jit(solution)/shard_map/all_to_all | solution.py:328
  173.6 17.6 %all_to_all.44 = bf16[16,32,128]{2,1,0:T(8,128)(2,1)S(1)} all-to-all(bf16[16,32,128]{2,1,0:T(8,128)(2,1)S(1)} %broadcast_in_dim.68), channel_id=1, replica_groups=mesh['z_hi'=4,'core'=2,'y'=4,'z_lo'=4,'x'=4] {'z_hi','z_lo'}, dimensions={0} | all-to-all | bytes 262144 | tf_op jit(solution)/shard_map/all_to_all | solution.py:324
  192.0 7.4 %all-to-all-start.7 = ((bf16[32,32,128]{2,1,0:T(8,128)(2,1)}), bf16[32,32,128]{2,1,0:T(8,128)(2,1)S(1)}, u32[]{:S(2)}, u32[]{:S(2)}) async-start(bf16[32,32,128]{2,1,0:T(8,128)(2,1)} %broadcast_in_dim.69), calls=%async_computation.7 | async-start | bytes 524288 | tf_op jit(solution)/shard_map/all_to_all | solution.py:324
  200.6 7.1 %all-to-all-done.7 = bf16[32,32,128]{2,1,0:T(8,128)(2,1)S(1)} async-done(((bf16[32,32,128]{2,1,0:T(8,128)(2,1)}), bf16[32,32,128]{2,1,0:T(8,128)(2,1)S(1)}, u32[]{:S(2)}, u32[]{:S(2)}) %all-to-all-start.7) | async-done | bytes 262176 | tf_op jit(solution)/shard_map/all_to_all | solution.py:324
  (60 shorter events, 14.3 us)
Async XLA Ops:
  33.1 4.7 %copy-start = (bf16[1,512,1024]{2,1,0:T(8,128)(2,1)S(1)}, bf16[1,512,1024]{2,1,0:T(8,128)(2,1)}, u32[]{:S(2)}) copy-start(bf16[1,512,1024]{2,1,0:T(8,128)(2,1)} %param.11) | copy-start | bytes 3145732
  33.1 41.0 %all-to-all-start.2 = ((bf16[4,4,4,16,1152]{4,3,2,1,0:T(8,128)(2,1)}), bf16[4,4,4,16,1152]{4,3,2,1,0:T(8,128)(2,1)}, u32[]{:S(2)}, u32[]{:S(2)}) async-start(bf16[4,4,4,16,1152]{4,3,2,1,0:T(8,128)(2,1)} %broadcast_in_dim.26), calls=%async_computation.2 | async-start | bytes 4718592 | tf_op jit(solution)/shard_map/all_to_all | solution.py:324
  37.8 11.3 %collective-permute-start.1 = (bf16[256,1024]{1,0:T(8,128)(2,1)S(1)}, bf16[256,1024]{1,0:T(8,128)(2,1)S(1)}, u32[]{:S(2)}, u32[]{:S(2)}) collective-permute-start(bf16[256,1024]{1,0:T(8,128)(2,1)S(1)} %get-tuple-element.42), channel_id=1, source_target_pairs={{1,0},{2,1},{3,2},{4,3},{5,4},{6,5},{7,6},{8,7},{9,8},{10,9},{11,1... | collective-permute-start | bytes 1572872 | tf_op jit(solution)/shard_map/ppermute | solution.py:344
  39.1 10.8 %collective-permute-start = (bf16[256,1024]{1,0:T(8,128)(2,1)S(1)}, bf16[256,1024]{1,0:T(8,128)(2,1)S(1)}, u32[]{:S(2)}, u32[]{:S(2)}) collective-permute-start(bf16[256,1024]{1,0:T(8,128)(2,1)S(1)} %get-tuple-element.43), channel_id=1, source_target_pairs={{0,1},{1,2},{2,3},{3,4},{4,5},{5,6},{6,7},{7,8},{8,9},{9,10},{10,1... | collective-permute-start | bytes 1572872 | tf_op jit(solution)/shard_map/ppermute | solution.py:343
  49.1 0.8 copy-start.9
  49.9 0.8 copy-start.11
  75.6 10.7 %copy-start.13 = (bf16[1024]{0:T(1024)(128)(2,1)S(1)}, bf16[1024]{0:T(1024)(128)(2,1)}, u32[]{:S(2)}) copy-start(bf16[1024]{0:T(1024)(128)(2,1)} %param.12) | copy-start | bytes 6148
  75.6 10.7 %copy-start.14 = (f32[16]{0:T(128)S(1)}, f32[16]{0:T(128)}, u32[]{:S(2)}) copy-start(f32[16]{0:T(128)} %param.17) | copy-start | bytes 196
  75.6 11.6 %collective-permute-start.2 = (bf16[4,4,4,16,1152]{4,3,2,1,0:T(8,128)(2,1)}, bf16[4,4,4,16,1152]{4,3,2,1,0:T(8,128)(2,1)}, u32[]{:S(2)}, u32[]{:S(2)}) collective-permute-start(bf16[4,4,4,16,1152]{4,3,2,1,0:T(8,128)(2,1)} %all-to-all-done.2.gathered_mine), channel_id=1, source_target_pairs={{0,64},{64,0},{1,65},{65,1},{2,66},{66,2},{3,67},{67,3},{4,68},{68... | collective-permute-start | bytes 7077896 | tf_op jit(solution)/shard_map/ppermute | solution.py:316
  82.7 27.2 %all-to-all-start.3 = ((bf16[4,4,4,16,896]{4,3,2,1,0:T(8,128)(2,1)}), bf16[4,4,4,16,896]{4,3,2,1,0:T(8,128)(2,1)S(1)}, u32[]{:S(2)}, u32[]{:S(2)}) async-start(bf16[4,4,4,16,896]{4,3,2,1,0:T(8,128)(2,1)} %broadcast_in_dim.27), calls=%async_computation.3 | async-start | bytes 3670016 | tf_op jit(solution)/shard_map/all_to_all | solution.py:361
  87.2 1.0 copy-start.10
  88.2 1.0 copy-start.12
  89.3 26.8 %copy-start.6 = (bf16[100,1024]{1,0:T(8,128)(2,1)S(1)}, bf16[100,1024]{1,0:T(8,128)(2,1)}, u32[]{:S(2)}) copy-start(bf16[100,1024]{1,0:T(8,128)(2,1)} %w_dec.1) | copy-start | bytes 614404
  103.4 1.3 copy-start.1
  104.8 1.0 copy-start.3
  109.9 6.1 %collective-permute-start.3 = (bf16[4,4,4,16,896]{4,3,2,1,0:T(8,128)(2,1)S(1)}, bf16[4,4,4,16,896]{4,3,2,1,0:T(8,128)(2,1)S(1)}, u32[]{:S(2)}, u32[]{:S(2)}) collective-permute-start(bf16[4,4,4,16,896]{4,3,2,1,0:T(8,128)(2,1)S(1)} %all-to-all-done.3.gathered_mine), channel_id=1, source_target_pairs={{0,64},{64,0},{1,65},{65,1},{2,66},{66,2},{3,67},{67,3},{4,68},{68... | collective-permute-start | bytes 5505032 | tf_op jit(solution)/shard_map/ppermute | solution.py:316
  116.0 1.6 copy-start.2
  117.6 1.2 copy-start.4
  118.9 40.6 %copy-start.5 = (bf16[100,1024]{1,0:T(8,128)(2,1)S(1)}, bf16[100,1024]{1,0:T(8,128)(2,1)}, u32[]{:S(2)}) copy-start(bf16[100,1024]{1,0:T(8,128)(2,1)} %targets.1) | copy-start | bytes 614404
  118.9 40.6 %copy-start.7 = (s32[1024]{0:T(1024)S(1)}, s32[1024]{0:T(1024)}, u32[]{:S(2)}) copy-start(s32[1024]{0:T(1024)} %param.20) | copy-start | bytes 12292
  118.9 40.6 %copy-start.8 = (f32[1024]{0:T(1024)S(1)}, f32[1024]{0:T(1024)}, u32[]{:S(2)}) copy-start(f32[1024]{0:T(1024)} %param.21) | copy-start | bytes 12292
  156.4 4.7 %collective-permute-start.4 = (bf16[4,25,16,128]{3,2,1,0:T(8,128)(2,1)S(1)}, bf16[4,25,16,128]{3,2,1,0:T(8,128)(2,1)S(1)}, u32[]{:S(2)}, u32[]{:S(2)}) collective-permute-start(bf16[4,25,16,128]{3,2,1,0:T(8,128)(2,1)S(1)} %all_to_all.42.same_core), channel_id=1, source_target_pairs={{0,64},{64,0},{1,65},{65,1},{2,66},{66,2},{3,67},{67,3},{4,68},{68... | collective-permute-start | bytes 1228808 | tf_op jit(solution)/shard_map/ppermute | solution.py:316
  192.0 15.7 %all-to-all-start.7 = ((bf16[32,32,128]{2,1,0:T(8,128)(2,1)}), bf16[32,32,128]{2,1,0:T(8,128)(2,1)S(1)}, u32[]{:S(2)}, u32[]{:S(2)}) async-start(bf16[32,32,128]{2,1,0:T(8,128)(2,1)} %broadcast_in_dim.69), calls=%async_computation.7 | async-start | bytes 524288 | tf_op jit(solution)/shard_map/all_to_all | solution.py:324
